TPU v7x, 32 devices: a whole 2x2x4 slice. The times are simulated.
32 devices in a mesh: section: 2 (over y), dp: 16 (over z, x, core).
Axes of the slice: x: 2, y: 2, z: 4, core: 2. Of those that a mesh axis runs over, the one named last changes fastest.
Arguments:
- x_in: bfloat16 [2, 4096, 1536], P(None, 'dp'), may hold values from -12 to 12
- lengths: int32 [2, 16, 2], P(None, 'dp'), may hold values from 1 to 255, as said below
- norm_pre: bfloat16 [2, 1536], P('section', 'dp'), may hold values from 0.5 to 1.5
- w_in: bfloat16 [2, 1536, 6448], P('section', 'dp'), may hold values from -0.15625 to 0.15625
- conv_w: bfloat16 [2, 4, 3328], P('section', None, 'dp'), may hold values from -0.59765625 to 0.59765625
- conv_b: bfloat16 [2, 3328], P('section', 'dp'), may hold values from -0.29882812 to 0.29882812
- dt_bias: float32 [2, 48], P('section'), may hold values from -5 to -2
- a_log: float32 [2, 48], P('section'), may hold values from 0 to 2.7
- skip_scale: float32 [2, 48], P('section'), may hold values from 0.5 to 1.5
- norm_gate: bfloat16 [2, 3072], P('section', 'dp'), may hold values from 0.5 to 1.5
- w_out: bfloat16 [2, 3072, 1536], P('section', None, 'dp'), may hold values from -0.109375 to 0.109375
- cotangent: bfloat16 [2, 4096, 1536], P(None, 'dp'), may hold values from -6 to 6
Outputs:
- outputs: float32 [2, 2, 4096, 1536], P('section', None, 'dp')
- in_grad: float32 [2, 2, 4096, 1536], P('section', None, 'dp')
- grad_norm_pre: float32 [2, 1536], P('section', 'dp')
- grad_w_in: float32 [2, 1536, 6448], P('section', 'dp')
- grad_conv_w: float32 [2, 4, 3328], P('section', None, 'dp')
- grad_conv_b: float32 [2, 3328], P('section', 'dp')
- grad_dt_bias: float32 [2, 48], P('section')
- grad_a_log: float32 [2, 48], P('section')
- grad_skip: float32 [2, 48], P('section')
- grad_norm_gate: float32 [2, 3072], P('section', 'dp')
- grad_w_out: float32 [2, 3072, 1536], P('section', None, 'dp')
- rms_stats: float32 [2, 2], P('section')
Inputs may be any that keep to these rules, and one draw needn't show every extreme that they name: Row [m, j] gives the lengths of the two sequences that fill slot j of micro-batch m from its first token on, back to back; the slot's tokens after them are padding. Together they cover 256 / 2 tokens or more. In every micro-batch some slot is full and holds one sequence of a single token and one of 255 tokens.
All inputs are finite; a program needn't handle non-finite values.
Results may differ from a plain program's by a relative error of at most 0.0083.
The roundings to bfloat16 on the way count: a program that leaves them out, or rounds other values in their place, can miss the bound.
Values may be sent and summed in bfloat16 or wider, within the bound.
A program may use at most 320 MiB of HBM per device.

v0:
```python
import jax
import jax.numpy as jnp
from jax import lax
from jax.sharding import PartitionSpec as P

epsilon = 1e-05
highest = lax.Precision.HIGHEST


def passed_along(shard, axis, by):
    length = lax.axis_size(axis)
    pairs = [(i, i + by) for i in range(length) if 0 <= i + by < length]
    return lax.ppermute(shard, axis, pairs)


def prenorm(resid, gain_vec):
    return resid * lax.rsqrt(jnp.mean(resid * resid, axis=-1, keepdims=True) + epsilon) * gain_vec


def segment_info(seq_lens, row_count):
    position = jnp.arange(row_count, dtype=jnp.int32)
    first_end = seq_lens[..., 0:1]
    second_end = first_end + seq_lens[..., 1:2]
    segment = (position >= first_end).astype(jnp.int32) + (position >= second_end).astype(jnp.int32)
    return (segment, position < second_end)


def mixer_core(projected, conv_wt, conv_bias, dt_shift, decay_log, skip_gain, gate_gain, segment):
    row_count = projected.shape[0]
    inner_width = gate_gain.shape[0]
    conv_width = conv_bias.shape[0]
    state_width = (conv_width - inner_width) // 2
    head_count = dt_shift.shape[0]
    kernel_len = conv_wt.shape[0]
    gate_in = projected[:, :inner_width]
    conv_in = projected[:, inner_width : inner_width + conv_width]
    dt_raw = projected[:, inner_width + conv_width :]
    conv_sum = conv_bias + conv_wt[kernel_len - 1] * conv_in
    for lag in range(1, kernel_len):
        earlier = jnp.concatenate(
            [jnp.zeros((lag, conv_width), conv_in.dtype), conv_in[:-lag]], axis=0
        )
        same_seg = jnp.concatenate([segment[:lag] < 0, segment[lag:] == segment[:-lag]])
        conv_sum = conv_sum + conv_wt[kernel_len - 1 - lag] * jnp.where(
            same_seg[:, None], earlier, 0.0
        )
    activated = jax.nn.silu(conv_sum)
    head_in = activated[:, :inner_width].reshape(row_count, head_count, -1)
    b_proj = activated[:, inner_width : inner_width + state_width]
    c_proj = activated[:, inner_width + state_width :]
    step_size = jax.nn.softplus(dt_raw + dt_shift)
    log_decay = jnp.cumsum(step_size * -jnp.exp(decay_log), axis=0).T
    position = jnp.arange(row_count)
    causal = (position[:, None] >= position[None, :]) & (segment[:, None] == segment[None, :])
    spread_gap = log_decay[:, :, None] - log_decay[:, None, :]
    decay_mat = jnp.where(causal[None], jnp.exp(jnp.where(causal[None], spread_gap, 0.0)), 0.0)
    c_dot_b = jnp.dot(c_proj, b_proj.T, precision=highest)
    mixing = decay_mat * c_dot_b[None] * step_size.T[:, None, :]
    mixed = (
        jnp.einsum("hts,shp->thp", mixing, head_in, precision=highest)
        + skip_gain[:, None] * head_in
    )
    gated = mixed.reshape(row_count, inner_width) * jax.nn.silu(gate_in)
    return prenorm(gated, gate_gain)


def contract_last(left_op, right_op):
    return lax.dot_general(
        left_op, right_op, (((1,), (1,)), ((), ())), preferred_element_type=jnp.float32
    )


def contract_first(left_op, right_op):
    return lax.dot_general(
        left_op, right_op, (((0,), (0,)), ((), ())), preferred_element_type=jnp.float32
    )


def add_tuples(total, addend):
    if total is None:
        return addend
    return tuple((held + extra for held, extra in zip(total, addend)))


def shards(
    x_in,
    lengths,
    norm_pre,
    w_in,
    conv_w,
    conv_b,
    dt_bias,
    a_log,
    skip_scale,
    norm_gate,
    w_out,
    cotangent,
):
    section_id = lax.axis_index("section")
    micro_count, row_count, model_width = x_in.shape
    gathered = (
        lax.all_gather(norm_pre[0], "dp", axis=0, tiled=True),
        lax.all_gather(w_in[0], "dp", axis=0, tiled=True),
        lax.all_gather(conv_w[0], "dp", axis=1, tiled=True),
        lax.all_gather(conv_b[0], "dp", axis=0, tiled=True),
        lax.all_gather(norm_gate[0], "dp", axis=0, tiled=True),
        lax.all_gather(w_out[0], "dp", axis=1, tiled=True),
    )
    shift_par = dt_bias[0]
    log_par = a_log[0]
    skip_par = skip_scale[0]
    segments, valid = segment_info(lengths[:, 0, :], row_count)
    valid_f = valid.astype(jnp.float32)
    gain_pre, in_proj, conv_wt, conv_bias, gate_gain, out_proj = gathered
    gain_f32 = gain_pre.astype(jnp.float32)
    conv_f32 = conv_wt.astype(jnp.float32)
    bias_f32 = conv_bias.astype(jnp.float32)
    gate_f32 = gate_gain.astype(jnp.float32)
    outgoing = jnp.zeros((row_count, model_width), jnp.float32)
    results = []
    saved = []
    resid_sq = jnp.zeros((), jnp.float32)
    branch_sq = jnp.zeros((), jnp.float32)
    valid_total = jnp.zeros((), jnp.float32)
    for step_no in range(micro_count + 1):
        received = passed_along(outgoing, "section", 1)
        micro_idx = step_no - section_id
        is_live = ((micro_idx >= 0) & (micro_idx < micro_count)).astype(jnp.float32)
        clipped = jnp.clip(micro_idx, 0, micro_count - 1)
        resid = jnp.where(
            section_id == 0, x_in[min(step_no, micro_count - 1)].astype(jnp.float32), received
        )
        segment = lax.dynamic_index_in_dim(segments, clipped, 0, keepdims=False)
        row_mask = lax.dynamic_index_in_dim(valid_f, clipped, 0, keepdims=False) * is_live
        normed_in = prenorm(resid, gain_f32).astype(jnp.bfloat16)
        projected = jnp.dot(normed_in, in_proj, preferred_element_type=jnp.float32)
        normed_out = mixer_core(
            projected, conv_f32, bias_f32, shift_par, log_par, skip_par, gate_f32, segment
        ).astype(jnp.bfloat16)
        branch = jnp.dot(normed_out, out_proj, preferred_element_type=jnp.float32)
        outgoing = resid + branch
        results.append(outgoing)
        saved.append((resid, normed_in, projected, normed_out, segment))
        resid_sq = resid_sq + jnp.sum(row_mask[:, None] * resid * resid)
        branch_sq = branch_sq + jnp.sum(row_mask[:, None] * branch * branch)
        valid_total = valid_total + jnp.sum(row_mask)
    totals = lax.psum((resid_sq, branch_sq, valid_total), "dp")
    rms_stats = jnp.stack(
        [
            jnp.sqrt(totals[0] / (totals[2] * model_width)),
            jnp.sqrt(totals[1] / (totals[2] * model_width)),
        ]
    )[None]
    outputs = jnp.stack(
        [
            jnp.where(section_id == 0, results[micro_no], results[micro_no + 1])
            for micro_no in range(micro_count)
        ]
    )[None]
    saved_resid = jnp.stack([entry[0] for entry in saved])
    saved_normed_in = jnp.stack([entry[1] for entry in saved])
    saved_projected = jnp.stack([entry[2] for entry in saved])
    saved_normed_out = jnp.stack([entry[3] for entry in saved])
    saved_segment = jnp.stack([entry[4] for entry in saved])
    back_weights = (
        lax.all_gather(norm_pre[0], "dp", axis=0, tiled=True),
        lax.all_gather(w_in[0], "dp", axis=0, tiled=True),
        lax.all_gather(conv_w[0], "dp", axis=1, tiled=True),
        lax.all_gather(conv_b[0], "dp", axis=0, tiled=True),
        lax.all_gather(norm_gate[0], "dp", axis=0, tiled=True),
        lax.all_gather(w_out[0], "dp", axis=1, tiled=True),
    )
    back_gain, back_in, back_conv, back_bias, back_gate, back_out = back_weights
    back_gain_f32 = back_gain.astype(jnp.float32)
    back_conv_f32 = back_conv.astype(jnp.float32)
    back_bias_f32 = back_bias.astype(jnp.float32)
    back_gate_f32 = back_gate.astype(jnp.float32)
    grad_back = jnp.zeros((row_count, model_width), jnp.float32)
    grad_results = []
    full_sums = None
    rate_sums = None
    normed_in_list = []
    normed_out_list = []
    proj_grads = []
    branch_grads = []
    for step_no in range(micro_count + 1):
        received = passed_along(grad_back.astype(jnp.bfloat16), "section", -1).astype(
            grad_back.dtype
        )
        micro_idx = step_no - 1 + section_id
        is_live = ((micro_idx >= 0) & (micro_idx < micro_count)).astype(jnp.float32)
        clipped = jnp.clip(micro_idx, 0, micro_count - 1)
        saved_idx = jnp.clip(step_no - 1 + 2 * section_id, 0, micro_count)
        resid = lax.dynamic_index_in_dim(saved_resid, saved_idx, 0, keepdims=False)
        normed_in = lax.dynamic_index_in_dim(saved_normed_in, saved_idx, 0, keepdims=False)
        projected = lax.dynamic_index_in_dim(saved_projected, saved_idx, 0, keepdims=False)
        normed_out = lax.dynamic_index_in_dim(saved_normed_out, saved_idx, 0, keepdims=False)
        segment = lax.dynamic_index_in_dim(saved_segment, saved_idx, 0, keepdims=False)
        seed_grad = lax.dynamic_index_in_dim(cotangent, clipped, 0, keepdims=False).astype(
            jnp.float32
        )
        seed_grad = (
            seed_grad * lax.dynamic_index_in_dim(valid_f, clipped, 0, keepdims=False)[:, None]
        )
        upstream = jnp.where(section_id == 1, seed_grad, received) * is_live
        grad_branch = upstream.astype(jnp.bfloat16)
        grad_normed = contract_last(grad_branch, back_out)

        def core_of(projected_in, conv_part, bias_part, gate_part, shift_part, log_part, skip_part):
            return mixer_core(
                projected_in,
                conv_part,
                bias_part,
                shift_part,
                log_part,
                skip_part,
                gate_part,
                segment,
            )

        core_pull = jax.vjp(
            core_of,
            projected,
            back_conv_f32,
            back_bias_f32,
            back_gate_f32,
            shift_par,
            log_par,
            skip_par,
        )[1]
        core_grads = core_pull(grad_normed)
        grad_proj = core_grads[0].astype(jnp.bfloat16)
        grad_normed_in = contract_last(grad_proj, back_in)
        norm_pull = jax.vjp(prenorm, resid, back_gain_f32)[1]
        grad_resid, grad_gain = norm_pull(grad_normed_in)
        grad_back = upstream + grad_resid
        grad_results.append(grad_back)
        rate_sums = add_tuples(rate_sums, (core_grads[4], core_grads[5], core_grads[6]))
        full_sums = add_tuples(full_sums, (grad_gain, core_grads[1], core_grads[2], core_grads[3]))
        normed_in_list.append(normed_in)
        normed_out_list.append(normed_out)
        proj_grads.append(grad_proj)
        branch_grads.append(grad_branch)
    weight_in_grad = contract_first(
        jnp.concatenate(normed_in_list, axis=0), jnp.concatenate(proj_grads, axis=0)
    )
    weight_out_grad = contract_first(
        jnp.concatenate(normed_out_list, axis=0), jnp.concatenate(branch_grads, axis=0)
    )
    row_shards = (
        lax.psum_scatter(full_sums[0], "dp", scatter_dimension=0, tiled=True),
        lax.psum_scatter(weight_in_grad, "dp", scatter_dimension=0, tiled=True),
        lax.psum_scatter(full_sums[2], "dp", scatter_dimension=0, tiled=True),
        lax.psum_scatter(full_sums[3], "dp", scatter_dimension=0, tiled=True),
    )
    col_shards = (
        lax.psum_scatter(full_sums[1], "dp", scatter_dimension=1, tiled=True),
        lax.psum_scatter(weight_out_grad, "dp", scatter_dimension=1, tiled=True),
    )
    rate_totals = lax.psum(rate_sums, "dp")
    in_grad = jnp.stack(
        [
            jnp.where(section_id == 1, grad_results[micro_no], grad_results[micro_no + 1])
            for micro_no in range(micro_count)
        ]
    )[None]
    return (
        outputs,
        in_grad,
        row_shards[0][None],
        row_shards[1][None],
        col_shards[0][None],
        row_shards[2][None],
        rate_totals[0][None],
        rate_totals[1][None],
        rate_totals[2][None],
        row_shards[3][None],
        col_shards[1][None],
        rms_stats,
    )


def solution(mesh):
    placed = (
        P(None, "dp", None),
        P(None, "dp", None),
        P("section", "dp"),
        P("section", "dp", None),
        P("section", None, "dp"),
        P("section", "dp"),
        P("section", None),
        P("section", None),
        P("section", None),
        P("section", "dp"),
        P("section", None, "dp"),
        P(None, "dp", None),
    )
    return jax.shard_map(
        shards,
        mesh=mesh,
        in_specs=placed,
        out_specs=(
            P("section", None, "dp", None),
            P("section", None, "dp", None),
            P("section", "dp"),
            P("section", "dp", None),
            P("section", None, "dp"),
            P("section", "dp"),
            P("section", None),
            P("section", None),
            P("section", None),
            P("section", "dp"),
            P("section", None, "dp"),
            P("section", None),
        ),
        check_vma=False,
    )
```

profile of v0, /device:TPU:0, one launch (start us, length us, event | category | flops | bytes accessed | tf_op | source)
XLA Modules:
  0.0 1574.0 jit_solution(16278350867582534574)
XLA Ops:
  18.4 62.8 %all-reduce.64 = (bf16[1536]{0:T(1024)(128)(2,1)S(1)}, bf16[3328]{0:T(1024)(128)(2,1)S(1)}, bf16[3072]{0:T(1024)(128)(2,1)S(1)}) all-reduce(bf16[1536]{0:T(1024)(128)(2,1)S(1)} %dynamic-update-slice.1, bf16[3328]{0:T(1024)(128)(2,1)S(1)} %dynamic-update-slice, ...), channel_id=4, replica_groups=mesh['section'=2,'dp'=16] {'dp'}, use_global_device_ids=true, to_apply=%add.58 | all-reduce | flops 7936 | bytes 31744
  81.4 36.1 %all-gather.1 = bf16[1,4,3328]{1,0,2:T(2,128)(2,1)S(1)} all-gather(bf16[1,4,208]{1,0,2:T(2,128)(2,1)S(1)} %copy.113), channel_id=3, replica_groups=mesh['section'=2,'dp'=16] {'dp'}, dimensions={2}, use_global_device_ids=true | all-gather | bytes 28288 | tf_op jit(solution)/shard_map/all_gather | solution.py:104
  129.6 69.9 %slice_reduce_fusion.3 = (f32[3328]{0:T(1024)S(1)}, f32[3328]{0:T(1024)S(1)}, f32[3328]{0:T(1024)S(1)}, f32[3328]{0:T(1024)S(1)}) fusion(f32[1,4,3328]{1,0,2:T(1,128)S(1)} %convert_element_type.173), kind=kLoop, calls=%fused_computation.312 | loop fusion | bytes 106496 | tf_op jit(solution)/shard_map/slice | solution.py:38
  200.9 15.3 fusion.10
  234.2 17.5 %bitcast_add_fusion.8 = f32[256,48,64]{0,2,1:T(8,128)S(1)} fusion(f32[256,48,64]{0,2,1:T(8,128)} %bitcast.559, f32[48,256]{1,0:T(8,128)} %get-tuple-element.177, f32[256,256]{1,0:T(8,128)S(1)} %fusion.252, f32[48,256]{1,0:T(8,128)S(1)} %copy_bitcast_fusion.5, pred[256,256]{1,0:T(8,128)(4,1)} %fusion.245, f32[48]{0:T(128)} %bitcast.599), kind=kOutput, calls=%fused_computation.262 | convolution fusion | flops 2433220608 | bytes 6717632 | tf_op jit(solution)/shard_map/hts,shp->thp/dot_general | solution.py:60
  275.1 26.6 %collective-permute-done.1 = f32[256,1536]{1,0:T(8,128)S(1)} collective-permute-done((f32[256,1536]{1,0:T(8,128)}, f32[256,1536]{1,0:T(8,128)S(1)}, u32[]{:S(2)}, u32[]{:S(2)}) %collective-permute-start.1) | collective-permute-done | bytes 1572896 | tf_op jit(solution)/shard_map/ppermute | solution.py:13
  304.1 15.3 fusion.8
  333.3 17.2 %bitcast_add_fusion.7 = f32[256,48,64]{0,2,1:T(8,128)S(1)} fusion(f32[256,48,64]{0,2,1:T(8,128)} %bitcast.560, f32[48,256]{1,0:T(8,128)S(1)} %get-tuple-element.175, f32[256,256]{1,0:T(8,128)S(1)} %fusion.249, f32[48,256]{1,0:T(8,128)S(1)} %copy_bitcast_fusion.4, pred[256,256]{1,0:T(8,128)(4,1)S(1)} %fusion.244, f32[48]{0:T(128)S(1)} %bitcast.601), kind=kOutput, calls=%fused_computation.260 | convolution fusion | flops 2433220608 | bytes 6717632 | tf_op jit(solution)/shard_map/hts,shp->thp/dot_general | solution.py:60
  381.2 19.9 %collective-permute-done.2 = f32[256,1536]{1,0:T(8,128)} collective-permute-done((f32[256,1536]{1,0:T(8,128)}, f32[256,1536]{1,0:T(8,128)}, u32[]{:S(2)}, u32[]{:S(2)}) %collective-permute-start.2) | collective-permute-done | bytes 1572896 | tf_op jit(solution)/shard_map/ppermute | solution.py:13
  403.6 15.2 fusion.6
  418.9 15.5 pad_maximum_fusion
  462.7 13.9 fusion.165
  494.1 13.1 fusion.166
  514.1 15.5 bitcast_add_fusion.6
  535.3 17.2 %bitcast_add_fusion.5 = f32[256,48,64]{0,2,1:T(8,128)S(1)} fusion(f32[256,48,64]{0,2,1:T(8,128)} %bitcast.556, f32[48,256]{1,0:T(8,128)S(1)} %get-tuple-element.236, f32[256,256]{1,0:T(8,128)S(1)} %copy-done.70, f32[48,256]{1,0:T(8,128)S(1)} %copy_bitcast_fusion.2, pred[256,256]{1,0:T(8,128)(4,1)S(1)} %copy-done.91, f32[48]{0:T(128)S(1)} %bitcast.603), kind=kOutput, calls=%fused_computation.256 | convolution fusion | flops 2433220608 | bytes 6717632 | tf_op jit(solution)/shard_map/jvp(hts,shp->thp)/dot_general | solution.py:60
  576.4 23.4 %fusion.73 = (f32[48,256]{1,0:T(8,128)S(1)}, f32[48,256]{1,0:T(8,128)S(1)}, f32[48,256]{1,0:T(8,128)S(1)}, f32[256,256]{1,0:T(8,128)S(1)}) fusion(f32[48,256]{1,0:T(8,128)S(1)} %get-tuple-element.236, f32[256,256]{1,0:T(8,128)S(1)} %copy-done.71, f32[48,256]{1,0:T(8,128)S(1)} %copy_bitcast_fusion.2, pred[256,256]{1,0:T(8,128)(4,1)S(1)} %copy-done.91, ...), kind=kOutput, calls=%fused_computation.80 | convolution fusion | flops 2463002624 | bytes 7127040 | tf_op jit(solution)/shard_map/transpose(jvp(hts,shp->thp))/dot_general | solution.py:60
  608.7 12.6 bitcast_add_fusion.4
  653.5 12.5 fusion.233
  668.7 16.9 %bitcast_add_fusion.3 = f32[256,48,64]{0,2,1:T(8,128)S(1)} fusion(f32[256,48,64]{0,2,1:T(8,128)} %bitcast.554, f32[48,256]{1,0:T(8,128)S(1)} %copy-done.105, f32[256,256]{1,0:T(8,128)S(1)} %fusion.264, f32[48,256]{1,0:T(8,128)S(1)} %copy_bitcast_fusion.1, pred[256,256]{1,0:T(8,128)(4,1)S(1)} %copy-done.89, f32[48]{0:T(128)S(1)} %bitcast.605), kind=kOutput, calls=%fused_computation.252 | convolution fusion | flops 2433220608 | bytes 6717632 | tf_op jit(solution)/shard_map/jvp(hts,shp->thp)/dot_general | solution.py:60
  706.8 17.3 %bitcast_add_fusion.1 = f32[256,48,64]{0,2,1:T(8,128)S(1)} fusion(f32[256,48,64]{0,2,1:T(8,128)} %bitcast.552, f32[48,256]{1,0:T(8,128)} %get-tuple-element.167, f32[256,256]{1,0:T(8,128)S(1)} %fusion.257, f32[48,256]{1,0:T(8,128)S(1)} %copy_bitcast_fusion, pred[256,256]{1,0:T(8,128)(4,1)} %fusion.240, f32[48]{0:T(128)} %bitcast.600), kind=kOutput, calls=%fused_computation.248 | convolution fusion | flops 2433220608 | bytes 6717632 | tf_op jit(solution)/shard_map/jvp(hts,shp->thp)/dot_general | solution.py:60
  749.2 20.9 %fusion.75 = (f32[48,256]{1,0:T(8,128)S(1)}, f32[48,256]{1,0:T(8,128)S(1)}, f32[48,256]{1,0:T(8,128)}, f32[256,256]{1,0:T(8,128)S(1)}) fusion(f32[48,256]{1,0:T(8,128)S(1)} %copy-done.106, f32[256,256]{1,0:T(8,128)S(1)} %copy-done.69, f32[48,256]{1,0:T(8,128)S(1)} %copy-done.112, pred[256,256]{1,0:T(8,128)(4,1)S(1)} %copy-done.90, ...), kind=kOutput, calls=%fused_computation.82 | convolution fusion | flops 2463002624 | bytes 7127040 | tf_op jit(solution)/shard_map/transpose(jvp(hts,shp->thp))/dot_general | solution.py:60
  770.9 12.6 bitcast_add_fusion.2
  815.4 14.1 fusion.229
  844.2 12.1 collective-permute-done.5
  873.6 20.9 %fusion.77 = (f32[48,256]{1,0:T(8,128)}, f32[48,256]{1,0:T(8,128)}, f32[48,256]{1,0:T(8,128)}, f32[256,256]{1,0:T(8,128)S(1)}) fusion(f32[48,256]{1,0:T(8,128)S(1)} %copy-done.104, f32[256,256]{1,0:T(8,128)S(1)} %copy-done.67, f32[48,256]{1,0:T(8,128)S(1)} %copy-done.110, pred[256,256]{1,0:T(8,128)(4,1)S(1)} %copy-done.88, ...), kind=kOutput, calls=%fused_computation.84 | convolution fusion | flops 2463002624 | bytes 7127040 | tf_op jit(solution)/shard_map/transpose(jvp(hts,shp->thp))/dot_general | solution.py:60
  897.1 12.6 bitcast_add_fusion
  921.8 13.9 fusion.132
  961.4 24.6 %fusion.54 = f32[1536,6448]{1,0:T(8,128)} fusion(bf16[256,6448]{0,1:T(8,128)(2,1)} %add_convert_fusion, bf16[256,6448]{0,1:T(8,128)(2,1)} %copy-done.54, bf16[256,6448]{0,1:T(8,128)(2,1)S(1)} %copy-done.53, bf16[256,1536]{1,0:T(8,128)(2,1)} %get-tuple-element.182, bf16[256,1536]{1,0:T(8,128)(2,1)} %get-tuple-element.183, ...), kind=kOutput, calls=%fused_computation.61 | convolution fusion | flops 15249530880 | bytes 51879936 | tf_op jit(solution)/shard_map/dot_general | solution.py:74
  997.6 16.9 %fusion.225 = (f32[1536]{0:T(1024)S(1)}, f32[256]{0:T(256)S(1)}, f32[256,1536]{1,0:T(8,128)}) fusion(f32[3,256,1536]{2,1,0:T(8,128)} %copy-done.20, s32[]{:T(128)S(6)} %min.36, f32[256]{0:T(256)S(1)} %fusion.309, f32[1536]{0:T(1024)S(1)} %copy-done.74, bf16[256,6448]{0,1:T(8,128)(2,1)} %add_convert_fusion, ...), kind=kOutput, calls=%fused_computation.341 | convolution fusion | flops 5073270784 | bytes 26269700 | tf_op jit(solution)/shard_map/dot_general | solution.py:68
  1014.6 61.7 %all-reduce.63 = (f32[1536]{0:T(1024)S(1)}, f32[3328]{0:T(1024)S(1)}, f32[1,48]{1,0:T(1,128)}, f32[1,48]{1,0:T(1,128)}, f32[1,48]{1,0:T(1,128)}, /*index=5*/f32[...) all-reduce(f32[1536]{0:T(1024)S(1)} %add_add_fusion.9, ...), channel_id=8, replica_groups=mesh['section'=2,'dp'=16] {'dp'}, use_global_device_ids=true, to_apply=%region_51.53.clone | all-reduce | flops 8083 | bytes 64664
  1087.3 89.2 %reduce-scatter.8.cloned.1.call-done = f32[3072,96]{0,1:T(8,128)} async-done(((f32[3072,1536]{0,1:T(8,128)}), f32[3072,96]{0,1:T(8,128)}) %reduce-scatter.8.cloned.1.call-update) | async-done | bytes 1179664 | tf_op jit(solution)/shard_map/reduce_scatter | solution.py:258
  1176.6 390.5 %reduce-scatter.6.cloned.1.call-done = f32[96,6448]{1,0:T(8,128)} async-done(((f32[1536,6448]{1,0:T(8,128)}), f32[96,6448]{1,0:T(8,128)}) %reduce-scatter.6.cloned.1.call-update) | async-done | bytes 2476048 | tf_op jit(solution)/shard_map/reduce_scatter | solution.py:252
  (770 shorter events, 396.2 us)
Async XLA Ops:
  7.2 74.0 %copy-start.200 = (bf16[1,4,208]{2,1,0:T(4,128)(2,1)S(1)}, bf16[1,4,208]{2,1,0:T(4,128)(2,1)}, u32[]{:S(2)}) copy-start(bf16[1,4,208]{2,1,0:T(4,128)(2,1)} %param.17) | copy-start | bytes 4996
  7.2 193.7 %all-gather.9.cloned.1.call-start = ((), (), s32[]{:S(2)}) async-start(), calls=%async_computation.5 | async-start | bytes 21307392 | tf_op jit(solution)/shard_map/all_gather | solution.py:103
  8.0 246.8 %all-gather.11.cloned.1.call-start = ((), (), s32[]{:S(2)}) async-start(), calls=%async_computation.6 | async-start | bytes 10027008 | tf_op jit(solution)/shard_map/all_gather | solution.py:107
  8.7 110.6 %copy-start.182 = (s32[2,1,2]{2,1,0:T(1,128)S(1)}, s32[2,1,2]{2,1,0:T(1,128)}, u32[]{:S(2)}) copy-start(s32[2,1,2]{2,1,0:T(1,128)} %param.14) | copy-start | bytes 52
  8.7 119.6 %copy-start.218 = (f32[1,48]{1,0:T(1,128)S(1)}, f32[1,48]{1,0:T(1,128)}, u32[]{:S(2)}) copy-start(f32[1,48]{1,0:T(1,128)} %param.20) | copy-start | bytes 580
  8.7 1077.0 %reduce-scatter.10.cloned.1.call-start = ((), (), s32[]{:S(2)}) async-start(), calls=%async_computation.7 | async-start | bytes 1810432
  9.0 190.6 %collective-permute-start = (f32[256,1536]{1,0:T(8,128)S(1)}, f32[256,1536]{1,0:T(8,128)}, u32[]{:S(2)}, u32[]{:S(2)}) collective-permute-start(f32[256,1536]{1,0:T(8,128)S(1)} %broadcast.619), channel_id=1, source_target_pairs={{0,16},{1,17},{2,18},{3,19},{4,20},{5,21},{6,22},{7,23},{8,24},{9,... | collective-permute-start | bytes 4718600 | tf_op jit(solution)/shard_map/ppermute | solution.py:13
  81.2 119.7 %copy-start.72 = (f32[1536]{0:T(1024)}, f32[1536]{0:T(1024)S(1)}, u32[]{:S(2)}) copy-start(f32[1536]{0:T(1024)S(1)} %convert_element_type.177) | copy-start | bytes 18436
  127.0 72.5 %copy-start.124 = (s32[1,256]{1,0:T(1,128)}, s32[1,256]{1,0:T(1,128)S(1)}, u32[]{:S(2)}) copy-start(s32[1,256]{1,0:T(1,128)S(1)} %get-tuple-element.220) | copy-start | bytes 3076
  128.3 71.2 %copy-start.183 = (f32[1,256]{1,0:T(1,128)}, f32[1,256]{1,0:T(1,128)S(1)}, u32[]{:S(2)}) copy-start(f32[1,256]{1,0:T(1,128)S(1)} %get-tuple-element.233) | copy-start | bytes 3076
  129.6 69.9 %copy-start.52 = (bf16[2,256,1536]{2,1,0:T(8,128)(2,1)S(1)}, bf16[2,256,1536]{2,1,0:T(8,128)(2,1)}, u32[]{:S(2)}) copy-start(bf16[2,256,1536]{2,1,0:T(8,128)(2,1)} %param.13) | copy-start | bytes 4718596
  254.8 46.8 %copy-start.148 = (f32[1,256]{1,0:T(1,128)S(1)}, f32[1,256]{1,0:T(1,128)}, u32[]{:S(2)}) copy-start(f32[1,256]{1,0:T(1,128)} %get-tuple-element.231) | copy-start | bytes 3076
  265.2 36.4 %collective-permute-start.1 = (f32[256,1536]{1,0:T(8,128)}, f32[256,1536]{1,0:T(8,128)S(1)}, u32[]{:S(2)}, u32[]{:S(2)}) collective-permute-start(f32[256,1536]{1,0:T(8,128)} %get-tuple-element.185), channel_id=1, source_target_pairs={{0,16},{1,17},{2,18},{3,19},{4,20},{5,21},{6,22},{7,23},{8,24},{9,... | collective-permute-start | bytes 4718600 | tf_op jit(solution)/shard_map/ppermute | solution.py:13
  268.4 111.6 %collective-permute-start.3 = (bf16[256,1536]{1,0:T(8,128)(2,1)}, bf16[256,1536]{1,0:T(8,128)(2,1)S(1)}, u32[]{:S(2)}, u32[]{:S(2)}) collective-permute-start(bf16[256,1536]{1,0:T(8,128)(2,1)} %broadcast.628), channel_id=1, source_target_pairs={{16,0},{17,1},{18,2},{19,3},{20,4},{21,5},{22,6},{23,7},{24,8},{25... | collective-permute-start | bytes 2359304 | tf_op jit(solution)/shard_map/ppermute | solution.py:13
  273.0 189.7 %copy-start.151 = (pred[256]{0:T(512)(128)(4,1)}, pred[256]{0:T(512)(128)(4,1)S(1)}, u32[]{:S(2)}) copy-start(pred[256]{0:T(512)(128)(4,1)S(1)} %get-tuple-element.265) | copy-start | bytes 772
  273.0 189.7 %copy-start.153 = (pred[256]{0:T(512)(128)(4,1)}, pred[256]{0:T(512)(128)(4,1)S(1)}, u32[]{:S(2)}) copy-start(pred[256]{0:T(512)(128)(4,1)S(1)} %get-tuple-element.264) | copy-start | bytes 772
  355.4 45.7 %copy-start.142 = (f32[1,256]{1,0:T(1,128)S(1)}, f32[1,256]{1,0:T(1,128)}, u32[]{:S(2)}) copy-start(f32[1,256]{1,0:T(1,128)} %get-tuple-element.111) | copy-start | bytes 3076
  363.8 37.3 %collective-permute-start.2 = (f32[256,1536]{1,0:T(8,128)}, f32[256,1536]{1,0:T(8,128)}, u32[]{:S(2)}, u32[]{:S(2)}) collective-permute-start(f32[256,1536]{1,0:T(8,128)} %get-tuple-element.148), channel_id=1, source_target_pairs={{0,16},{1,17},{2,18},{3,19},{4,20},{5,21},{6,22},{7,23},{8,24},{9,... | collective-permute-start | bytes 4718600 | tf_op jit(solution)/shard_map/ppermute | solution.py:13
  368.9 50.0 %copy-start.162 = (pred[256]{0:T(512)(128)(4,1)}, pred[256]{0:T(512)(128)(4,1)S(1)}, u32[]{:S(2)}) copy-start(pred[256]{0:T(512)(128)(4,1)S(1)} %get-tuple-element.259) | copy-start | bytes 772
  368.9 50.0 %copy-start.169 = (pred[256]{0:T(512)(128)(4,1)}, pred[256]{0:T(512)(128)(4,1)S(1)}, u32[]{:S(2)}) copy-start(pred[256]{0:T(512)(128)(4,1)S(1)} %get-tuple-element.258) | copy-start | bytes 772
  444.2 48.7 %copy-start = (f32[256,6448]{0,1:T(8,128)}, f32[256,6448]{0,1:T(8,128)S(1)}, u32[]{:S(2)}) copy-start(f32[256,6448]{0,1:T(8,128)S(1)} %get-tuple-element.159) | copy-start | bytes 19808260
  444.2 48.7 %copy-start.1 = (f32[256,6448]{0,1:T(8,128)}, f32[256,6448]{0,1:T(8,128)S(1)}, u32[]{:S(2)}) copy-start(f32[256,6448]{0,1:T(8,128)S(1)} %get-tuple-element.160) | copy-start | bytes 19808260
  486.9 89.5 %copy-start.107 = (f32[48,256]{1,0:T(8,128)}, f32[48,256]{1,0:T(8,128)S(1)}, u32[]{:S(2)}) copy-start(f32[48,256]{1,0:T(8,128)S(1)} %get-tuple-element.236) | copy-start | bytes 147460
  602.8 65.3 %copy-start.68 = (f32[256,256]{1,0:T(8,128)}, f32[256,256]{1,0:T(8,128)S(1)}, u32[]{:S(2)}) copy-start(f32[256,256]{1,0:T(8,128)S(1)} %fusion.264) | copy-start | bytes 786436
  606.0 100.8 %copy-start.66 = (f32[256,256]{1,0:T(8,128)}, f32[256,256]{1,0:T(8,128)S(1)}, u32[]{:S(2)}) copy-start(f32[256,256]{1,0:T(8,128)S(1)} %fusion.257) | copy-start | bytes 786436
  704.1 26.3 %collective-permute-start.4 = (bf16[256,1536]{1,0:T(8,128)(2,1)}, bf16[256,1536]{1,0:T(8,128)(2,1)S(1)}, u32[]{:S(2)}, u32[]{:S(2)}) collective-permute-start(bf16[256,1536]{1,0:T(8,128)(2,1)} %get-tuple-element.201), channel_id=1, source_target_pairs={{16,0},{17,1},{18,2},{19,3},{20,4},{21,5},{22,6},{23,7},{24,8},{25... | collective-permute-start | bytes 2359304 | tf_op jit(solution)/shard_map/ppermute | solution.py:13
  833.8 22.5 %collective-permute-start.5 = (bf16[256,1536]{1,0:T(8,128)(2,1)S(1)}, bf16[256,1536]{1,0:T(8,128)(2,1)S(1)}, u32[]{:S(2)}, u32[]{:S(2)}) collective-permute-start(bf16[256,1536]{1,0:T(8,128)(2,1)S(1)} %convert_element_type.159), channel_id=1, source_target_pairs={{16,0},{17,1},{18,2},{19,3},{20,4},{21,5},{22,6},{23,7},{24,8},{25... | collective-permute-start | bytes 2359304 | tf_op jit(solution)/shard_map/ppermute | solution.py:13
  921.7 254.9 %reduce-scatter.8.cloned.1.call-start = ((), (), s32[]{:S(2)}) async-start(), calls=%async_computation.4 | async-start | bytes 20054016 | tf_op jit(solution)/shard_map/reduce_scatter | solution.py:258
  935.7 631.3 %reduce-scatter.6.cloned.1.call-start = ((), (), s32[]{:S(2)}) async-start(), calls=%async_computation.3 | async-start | bytes 42614784 | tf_op jit(solution)/shard_map/reduce_scatter | solution.py:252
  997.6 83.2 %copy-start.28 = (bf16[2,256,1536]{2,1,0:T(8,128)(2,1)S(1)}, bf16[2,256,1536]{2,1,0:T(8,128)(2,1)}, u32[]{:S(2)}) copy-start(bf16[2,256,1536]{2,1,0:T(8,128)(2,1)} %param.24) | copy-start | bytes 4718596
  997.6 83.2 %copy-start.30 = (f32[256,1536]{1,0:T(8,128)S(1)}, f32[256,1536]{1,0:T(8,128)}, u32[]{:S(2)}) copy-start(f32[256,1536]{1,0:T(8,128)} %copy-done.29) | copy-start | bytes 4718596
  997.6 83.2 %copy-start.130 = (f32[1,256]{1,0:T(1,128)S(1)}, f32[1,256]{1,0:T(1,128)}, u32[]{:S(2)}) copy-start(f32[1,256]{1,0:T(1,128)} %get-tuple-element.215) | copy-start | bytes 3076
  (222 other events, 2086.1 us)
Sparse Core Ops, SparseCore 0:
  9.7 124.3 all-gather.8
  136.3 81.5 all-gather.10
  921.8 56.4 reduce-scatter.9
  982.8 193.6 reduce-scatter.7
  1181.3 385.6 reduce-scatter.5
where the time goes:
time: 1580 us; the launch traced here: 1570 us
  waiting for transfers between devices  540 us (34%)
  matrix products  404 us (26%)
  other arithmetic  247 us (16%)
  local copies, waits for them, and re-layouts  171 us (11%)
  blocking collectives  161 us (10%)
  between operations  33.9 us (2%)
  starting transfers between devices  17.6 us (1%)
    reduce_scatter x1, waiting for transfers between devices, shards(): lax.psum_scatter(weight_in_grad, 'dp', scatter_dimension=0, tiled=True)  390 us
    dot_general x12, matrix products, mixer_core(): jnp.einsum('hts,shp->thp', mixing, head_in, precision=highest)  205 us
    unnamed x2, blocking collectives  125 us
    reduce_scatter x1, waiting for transfers between devices, shards(): lax.psum_scatter(weight_out_grad, 'dp', scatter_dimension=1, tiled=True)  89.2 us
    dot_general x6, matrix products, contract_last(): lax.dot_general(left_op, right_op, (((1,), (1,)), ((), ())), preferred_el...  74.3 us
    slice x1, local copies, waits for them, and re-layouts, mixer_core(): conv_sum = conv_bias + conv_wt[kernel_len - 1] * conv_in  69.9 us
    ppermute x6, waiting for transfers between devices, passed_along(): return lax.ppermute(shard, axis, pairs)  58.6 us
    dot_general x3, matrix products, shards(): projected = jnp.dot(normed_in, in_proj, preferred_element_type=jnp.float32)  45.9 us
  transfers between devices with their start and end apart: 11, of which 5 were waited for; matrix products, arithmetic and copies ran while one was open for 21% of the time, Pallas kernels for 0%

commit v1 on v0

v1 whole, which is shorter than its diff:
```python
import functools

import jax
import jax.numpy as jnp
from jax import lax
from jax.experimental import pallas as pl
from jax.experimental.pallas import tpu as pltpu
from jax.sharding import PartitionSpec as P

EPS = 1e-05
F32 = jnp.float32
BF16 = jnp.bfloat16
LANE = 128
LOG2E = 1.4426950408889634
NEG = -1e30
VMEM_LIMIT = 60 * 1024 * 1024
HIGH = lax.Precision.HIGHEST
IN_BLOCKS = 3
OUT_BLOCKS = 4
GN_BLOCKS = 4
GNI_BLOCKS = 6


def dot_nn(a, b, precision=None):
    return lax.dot_general(
        a, b, (((1,), (0,)), ((), ())), preferred_element_type=F32, precision=precision
    )


def dot_nt(a, b, precision=None):
    return lax.dot_general(
        a, b, (((1,), (1,)), ((), ())), preferred_element_type=F32, precision=precision
    )


def dot_tn(a, b, precision=None):
    return lax.dot_general(
        a, b, (((0,), (0,)), ((), ())), preferred_element_type=F32, precision=precision
    )


def sigmoid(v):
    return 1.0 / (1.0 + jnp.exp(-v))


def iota(shape, dim):
    return lax.broadcasted_iota(jnp.int32, shape, dim)


def row_sum(v):
    return jnp.sum(v, axis=1, keepdims=True)


def col_sum(v):
    return jnp.sum(v, axis=0, keepdims=True)


def segments_of(position, first_end, second_end):
    return (position >= first_end).astype(jnp.int32) + (position >= second_end).astype(jnp.int32)


def decay_terms(dt_raw, hp_ref, rows):
    z = dt_raw + hp_ref[0:1, :]
    step = jnp.maximum(z, 0.0) + jnp.log1p(jnp.exp(-jnp.abs(z)))
    below = (iota((rows, rows), 1) <= iota((rows, rows), 0)).astype(F32)
    ld = dot_nn(below, step * (hp_ref[1:2, :] * LOG2E), HIGH)
    lr = ld - jnp.log2(jnp.maximum(step, 1e-37))
    return z, step, ld, lr


def to_rows(v, out_ref, pairs):
    vt = v.T
    for p in range(pairs):
        out_ref[p, 0:2, :] = vt[2 * p : 2 * p + 2, :]


def pair_lanes(ref, p):
    return pltpu.roll(ref[...], lax.rem(LANE - 2 * p, LANE), 1)


def fwd_kernel(
    scal, x_ref, recv_ref, win_ref, wout_ref, par_ref, hp_ref, *rest
):
    (a0, a1, a2, a3, a4, a5, a6,
     nin_ref, nout_ref, out_ref, resid_ref, proj_hbm, csum_hbm, mixed_hbm, branch_ref, stat_ref,
     proj, csum, act, mixed, gated, ld_s, lr_t, cb, maskb, sem) = rest
    step = pl.program_id(0)
    rows, di, cw = gated.shape[0], gated.shape[1], csum.shape[1]
    half = rows // 2
    slot, e1, e2 = scal[1], scal[2], scal[3]
    in_cols = win_ref.shape[1]
    out_cols = wout_ref.shape[0]
    pairs = di // LANE
    copies = (
        pltpu.make_async_copy(proj, proj_hbm.at[slot], sem.at[0]),
        pltpu.make_async_copy(csum, csum_hbm.at[slot], sem.at[1]),
        pltpu.make_async_copy(mixed, mixed_hbm.at[slot], sem.at[2]),
    )

    @pl.when(step == 0)
    def _():
        u = x_ref[0].astype(F32) + recv_ref[...].astype(F32)
        q = lax.rsqrt(jnp.mean(u * u, axis=1, keepdims=True) + EPS)
        nin_ref[0] = (u * q * par_ref[7:8, : u.shape[1]]).astype(BF16)
        resid_ref[0] = u

    for i in range(IN_BLOCKS):

        @pl.when(step == i)
        def _():
            proj[:, i * in_cols : (i + 1) * in_cols] = dot_nn(nin_ref[0], win_ref[...])

    @pl.when(step == IN_BLOCKS)
    def _():
        copies[0].start()
        pos = iota((rows, LANE), 0)
        dist = pos - jnp.where(pos >= e2, e2, jnp.where(pos >= e1, e1, 0))

        def conv_tile(j, carry):
            off = pl.multiple_of(j * LANE, LANE)
            v = proj[:, pl.ds(pl.multiple_of(di + j * LANE, LANE), LANE)]
            acc = par_ref[4:5, pl.ds(off, LANE)] + par_ref[3:4, pl.ds(off, LANE)] * v
            for lag in range(1, 4):
                acc += par_ref[3 - lag : 4 - lag, pl.ds(off, LANE)] * jnp.where(
                    dist >= lag, pltpu.roll(v, lag, 0), 0.0
                )
            csum[:, pl.ds(off, LANE)] = acc
            act[:, pl.ds(off, LANE)] = acc * sigmoid(acc)
            return carry

        lax.fori_loop(0, cw // LANE, conv_tile, 0)
        copies[1].start()
        _, _, ld, lr = decay_terms(proj[:, di + cw :], hp_ref, rows)
        ld_s[...] = ld
        to_rows(lr, lr_t, pairs)
        cb[...] = dot_nt(act[:, di + LANE :], act[:, di : di + LANE], HIGH)
        rpos, cpos = iota((rows, rows), 0), iota((rows, rows), 1)
        keep = (rpos >= cpos) & (segments_of(rpos, e1, e2) == segments_of(cpos, e1, e2))
        maskb[...] = jnp.where(keep, 0.0, NEG)
        first = iota((rows, LANE), 1) < LANE // 2

        def pair(p, sq):
            off = pl.multiple_of(p * LANE, LANE)
            x = act[:, pl.ds(off, LANE)]
            ldr = pair_lanes(ld_s, p)
            y0 = jnp.zeros((half, LANE), F32)
            y1 = jnp.zeros((half, LANE), F32)
            for h in range(2):
                xm = jnp.where(first if h == 0 else ~first, x, 0.0).astype(BF16)
                lc = ldr[:, h : h + 1]
                lrow = lr_t[p, h : h + 1, :]
                m0 = jnp.exp2((lc[:half] - lrow[:, :half]) + maskb[:half, :half]) * cb[:half, :half]
                m1 = jnp.exp2((lc[half:] - lrow) + maskb[half:, :]) * cb[half:, :]
                y0 += dot_nn(m0.astype(BF16), xm[:half])
                y1 += dot_nn(m1.astype(BF16), xm)
            y = jnp.concatenate([y0, y1], axis=0) + par_ref[6:7, pl.ds(off, LANE)] * x
            mixed[:, pl.ds(off, LANE)] = y
            gate = proj[:, pl.ds(off, LANE)]
            g = y * (gate * sigmoid(gate))
            gated[:, pl.ds(off, LANE)] = g
            return sq + g * g

        sq = lax.fori_loop(0, pairs, pair, jnp.zeros((rows, LANE), F32))
        copies[2].start()
        r = lax.rsqrt(row_sum(sq) * (1.0 / di) + EPS)
        nout_ref[0] = (gated[...] * r * par_ref[5:6, :di]).astype(BF16)

    for i in range(OUT_BLOCKS):

        @pl.when(step == IN_BLOCKS + 1 + i)
        def _():
            cols = slice(i * out_cols, (i + 1) * out_cols)
            branch = dot_nt(nout_ref[0], wout_ref[...])
            u = resid_ref[0, :, cols]
            valid = iota((rows, 1), 0) < e2
            out_ref[0, :, cols] = u + branch
            branch_ref[:, cols] = branch.astype(BF16)
            usq = col_sum(row_sum(jnp.where(valid, u * u, 0.0)))
            bsq = col_sum(row_sum(jnp.where(valid, branch * branch, 0.0)))
            lane = iota((8, LANE), 1)
            part = jnp.where(lane == 0, usq, jnp.where(lane == 1, bsq, 0.0))
            if i == 0:
                stat_ref[...] = part
            else:
                stat_ref[...] += part

    @pl.when(step == IN_BLOCKS + OUT_BLOCKS)
    def _():
        for copy in copies:
            copy.wait()


def forward_step(scal, x_in, recv, w_in, w_out_t, par, hp, held):
    rows, d = recv.shape
    di = w_out_t.shape[1]
    wide = w_in.shape[1]
    cw = par.shape[1]
    in_cols, out_rows = wide // IN_BLOCKS, d // OUT_BLOCKS
    last = IN_BLOCKS + OUT_BLOCKS

    def stacked(width):
        return pl.BlockSpec((1, rows, width), lambda i, s: (s[1], 0, 0))

    any_spec = pl.BlockSpec(memory_space=pl.ANY)
    whole = lambda i, s: (0, 0)
    grid_spec = pltpu.PrefetchScalarGridSpec(
        num_scalar_prefetch=1,
        grid=(last + 1,),
        in_specs=[
            pl.BlockSpec((1, rows, d), lambda i, s: (s[0], 0, 0)),
            pl.BlockSpec((rows, d), whole),
            pl.BlockSpec((d, in_cols), lambda i, s: (0, jnp.minimum(i, IN_BLOCKS - 1))),
            pl.BlockSpec((out_rows, di), lambda i, s: (jnp.maximum(i - IN_BLOCKS - 1, 0), 0)),
            pl.BlockSpec(par.shape, whole),
            pl.BlockSpec(hp.shape, whole),
        ]
        + [any_spec] * 7,
        out_specs=[stacked(d), stacked(di), stacked(d), stacked(d)]
        + [any_spec] * 3
        + [pl.BlockSpec((rows, d), whole), pl.BlockSpec((8, LANE), whole)],
        scratch_shapes=[
            pltpu.VMEM((rows, wide), F32),
            pltpu.VMEM((rows, cw), F32),
            pltpu.VMEM((rows, cw), F32),
            pltpu.VMEM((rows, di), F32),
            pltpu.VMEM((rows, di), F32),
            pltpu.VMEM((rows, LANE), F32),
            pltpu.VMEM((di // LANE, 8, rows), F32),
            pltpu.VMEM((rows, rows), F32),
            pltpu.VMEM((rows, rows), F32),
            pltpu.SemaphoreType.DMA((3,)),
        ],
    )
    outs = pl.pallas_call(
        fwd_kernel,
        grid_spec=grid_spec,
        out_shape=[jax.ShapeDtypeStruct(v.shape, v.dtype) for v in held]
        + [jax.ShapeDtypeStruct((rows, d), BF16), jax.ShapeDtypeStruct((8, LANE), F32)],
        input_output_aliases={7 + k: k for k in range(7)},
        compiler_params=pltpu.CompilerParams(vmem_limit_bytes=VMEM_LIMIT),
        cost_estimate=pl.CostEstimate(
            flops=2 * rows * d * (wide + di), bytes_accessed=60 << 20, transcendentals=4 << 20
        ),
        name="mixer_forward",
    )(scal, x_in, recv, w_in, w_out_t, par, hp, *held)
    return outs[:7], outs[7], outs[8]


def bwd_kernel(scal, cot_ref, recv_ref, resid_ref, win_ref, wout_ref, par_ref, hp_ref, *rest):
    (proj_hbm, csum_hbm, mixed_hbm, a0, a1, a2,
     gproj_ref, gbr_ref, ing_ref, send_ref, pack_ref,
     proj, csum, mixed, gn, gni, act_bc, ld_t, lr_s, row_q, col_q, cbt, dcbt, maskb, stat, sem) = rest
    step = pl.program_id(0)
    rows, di, cw = mixed.shape[0], mixed.shape[1], csum.shape[1]
    d = gni.shape[1]
    half = rows // 2
    src, e1, e2, seeded = scal[1], scal[3], scal[4], scal[5]
    pairs = di // LANE
    gn_cols, gni_cols = wout_ref.shape[1], win_ref.shape[0]
    gate_in = pltpu.make_async_copy(
        proj_hbm.at[src, :, pl.ds(0, di)], proj.at[:, pl.ds(0, di)], sem.at[0]
    )
    mixed_in = pltpu.make_async_copy(mixed_hbm.at[src], mixed, sem.at[1])
    conv_in = pltpu.make_async_copy(
        proj_hbm.at[src, :, pl.ds(di, proj.shape[1] - di)],
        proj.at[:, pl.ds(di, proj.shape[1] - di)],
        sem.at[2],
    )
    csum_in = pltpu.make_async_copy(csum_hbm.at[src], csum, sem.at[3])

    @pl.when(step == 0)
    def _():
        for copy in (gate_in, mixed_in, csum_in, conv_in):
            copy.start()
        valid = (iota((rows, 1), 0) < e2).astype(F32) * seeded.astype(F32)
        g = cot_ref[0].astype(F32) * valid + recv_ref[...].astype(F32)
        ing_ref[0] = g
        gbr_ref[0] = g.astype(BF16)
        stat[...] = jnp.zeros_like(stat)
        pack_ref[...] = jnp.zeros_like(pack_ref)
        gate_in.wait()
        mixed_in.wait()

    for i in range(GN_BLOCKS):

        @pl.when(step == i)
        def _():
            base = i * gn_cols
            gn[:, base : base + gn_cols] = dot_nn(gbr_ref[0], wout_ref[...])

            def tile(j, carry):
                sq, cross = carry
                off = pl.multiple_of(base + j * LANE, LANE)
                gate = proj[:, pl.ds(off, LANE)]
                gated = mixed[:, pl.ds(off, LANE)] * (gate * sigmoid(gate))
                sq += gated * gated
                cross += gated * (par_ref[5:6, pl.ds(off, LANE)] * gn[:, pl.ds(off, LANE)])
                return sq, cross

            sq, cross = lax.fori_loop(0, gn_cols // LANE, tile, (stat[0], stat[1]))
            stat[0] = sq
            stat[1] = cross

    @pl.when(step == GN_BLOCKS)
    def _():
        csum_in.wait()
        conv_in.wait()
        r = lax.rsqrt(row_sum(stat[0]) * (1.0 / di) + EPS)
        rc = r * r * r * (row_sum(stat[1]) * (1.0 / di))
        stat[0] = jnp.broadcast_to(r, (rows, LANE))
        stat[1] = jnp.broadcast_to(rc, (rows, LANE))
        z, dt, ld, lr = decay_terms(proj[:, di + cw :], hp_ref, rows)
        lr_s[...] = lr
        to_rows(ld, ld_t, pairs)
        for j in range(2):
            v = csum[:, di + j * LANE : di + (j + 1) * LANE]
            act_bc[j] = v * sigmoid(v)
        cbt[...] = dot_nt(act_bc[0], act_bc[1], HIGH)
        rpos, cpos = iota((rows, rows), 0), iota((rows, rows), 1)
        keep = (rpos <= cpos) & (segments_of(rpos, e1, e2) == segments_of(cpos, e1, e2))
        maskb[...] = jnp.where(keep, 0.0, NEG)
        dcbt[...] = jnp.zeros_like(dcbt)
        col_q[...] = jnp.zeros_like(col_q)
        row_q[...] = jnp.zeros_like(row_q)
        lane = iota((rows, LANE), 1)
        first = lane < LANE // 2
        pos = iota((rows, LANE), 0)
        ahead = jnp.where(pos < e1, e1, jnp.where(pos < e2, e2, rows)) - pos

        def conv_back(dcv, off):
            here = pl.ds(off, LANE)
            v = proj[:, pl.ds(pl.multiple_of(di + off, LANE), LANE)]
            out = par_ref[3:4, here] * dcv
            pack_ref[3:4, here] = col_sum(dcv * v)
            pack_ref[4:5, here] = col_sum(dcv)
            for lag in range(1, 4):
                moved = jnp.where(ahead > lag, pltpu.roll(dcv, rows - lag, 0), 0.0)
                out += par_ref[3 - lag : 4 - lag, here] * moved
                pack_ref[3 - lag : 4 - lag, here] = col_sum(moved * v)
            gproj_ref[0, :, pl.ds(pl.multiple_of(di + off, LANE), LANE)] = out.astype(BF16)

        def pair(p, carry):
            off = pl.multiple_of(p * LANE, LANE)
            here = pl.ds(off, LANE)
            gate = proj[:, here]
            mx = mixed[:, here]
            gnt = gn[:, here]
            sg = sigmoid(gate)
            sil = gate * sg
            gated = mx * sil
            pack_ref[5:6, here] = col_sum(gated * stat[0] * gnt)
            gg = stat[0] * (par_ref[5:6, here] * gnt) - gated * stat[1]
            dy = gg * sil
            gproj_ref[0, :, here] = (gg * mx * (sg * (1.0 + gate * (1.0 - sg)))).astype(BF16)
            cs = csum[:, here]
            sc = sigmoid(cs)
            x = cs * sc
            pack_ref[6:7, here] = col_sum(dy * x)
            xb = x.astype(BF16)
            lrr = pair_lanes(lr_s, p)
            dx0 = jnp.zeros((half, LANE), F32)
            dx1 = jnp.zeros((half, LANE), F32)
            for h in range(2):
                mine = first if h == 0 else ~first
                dym = jnp.where(mine, dy, 0.0).astype(BF16)
                lc = lrr[:, h : h + 1]
                lrow = ld_t[p, h : h + 1, :]
                d0 = jnp.exp2((lrow - lc[:half]) + maskb[:half, :])
                d1 = jnp.exp2((lrow[:, half:] - lc[half:]) + maskb[half:, half:])
                t0 = dot_nt(xb[:half], dym) * d0
                t1 = dot_nt(xb[half:], dym[half:]) * d1
                dx0 += dot_nn((d0 * cbt[:half, :]).astype(BF16), dym)
                dx1 += dot_nn((d1 * cbt[half:, half:]).astype(BF16), dym[half:])
                dcbt[:half, :] += t0
                dcbt[half:, half:] += t1
                q0 = t0 * cbt[:half, :]
                q1 = t1 * cbt[half:, half:]
                row_q[p, h : h + 1, :half] = col_sum(q0[:, :half])
                row_q[p, h : h + 1, half:] = col_sum(q0[:, half:]) + col_sum(q1)
                picked = lane == 2 * p + h
                col_q[:half, :] = jnp.where(picked[:half], row_sum(q0), col_q[:half, :])
                col_q[half:, :] = jnp.where(picked[half:], row_sum(q1), col_q[half:, :])
            dx = jnp.concatenate([dx0, dx1], axis=0) + par_ref[6:7, here] * dy
            conv_back(dx * (sc * (1.0 + cs * (1.0 - sc))), off)
            return carry

        lax.fori_loop(0, pairs, pair, 0)
        dcb = dcbt[...]
        for j, grad in enumerate((dot_nn(dcb, act_bc[1], HIGH), dot_tn(dcb, act_bc[0], HIGH))):
            cs = csum[:, di + j * LANE : di + (j + 1) * LANE]
            sc = sigmoid(cs)
            conv_back(grad * (sc * (1.0 + cs * (1.0 - sc))), di + j * LANE)
        spread = jnp.concatenate(
            [row_q[p, 0:2, :] for p in range(pairs)]
            + [jnp.zeros((LANE - 2 * pairs, rows), F32)],
            axis=0,
        )
        colq = col_q[...]
        dld = spread.T - colq
        above = (iota((rows, rows), 1) >= iota((rows, rows), 0)).astype(F32)
        after = dot_nn(above, dld, HIGH)
        sz = sigmoid(z)
        ratio = jnp.where(z < -20.0, 1.0, sz / jnp.maximum(dt, 1e-37))
        neg_rate = hp_ref[1:2, :]
        ddt = jnp.where(lane < 2 * pairs, colq * ratio + neg_rate * after * sz, 0.0)
        gproj_ref[0, :, di + cw :] = ddt.astype(BF16)
        pack_ref[7:8, d : d + LANE] = col_sum(ddt)
        pack_ref[7:8, d + LANE : d + 2 * LANE] = col_sum(
            jnp.where(lane < 2 * pairs, neg_rate * dt * after, 0.0)
        )

    for i in range(GNI_BLOCKS):

        @pl.when(step == GN_BLOCKS + 1 + i)
        def _():
            gni[:, i * gni_cols : (i + 1) * gni_cols] = dot_nt(gproj_ref[0], win_ref[...])

    @pl.when(step == GN_BLOCKS + GNI_BLOCKS)
    def _():
        u = resid_ref[0]
        gi = gni[...]
        q = lax.rsqrt(jnp.mean(u * u, axis=1, keepdims=True) + EPS)
        w = par_ref[7:8, :d] * gi
        total = ing_ref[0] + q * w - u * (q * q * q * jnp.mean(u * w, axis=1, keepdims=True))
        ing_ref[0] = total
        send_ref[...] = total.astype(BF16)
        pack_ref[7:8, :d] = col_sum(u * q * gi)


def backward_step(scal, cot, recv, w_in, w_out_t, par, hp, resid, kept, held):
    rows, d = recv.shape
    di = w_out_t.shape[1]
    wide = w_in.shape[1]
    cw = par.shape[1]
    pairs = di // LANE
    gn_cols, gni_rows = di // GN_BLOCKS, d // GNI_BLOCKS
    last = GN_BLOCKS + GNI_BLOCKS

    def stacked(width, k):
        return pl.BlockSpec((1, rows, width), lambda i, s: (s[k], 0, 0))

    any_spec = pl.BlockSpec(memory_space=pl.ANY)
    whole = lambda i, s: (0, 0)
    grid_spec = pltpu.PrefetchScalarGridSpec(
        num_scalar_prefetch=1,
        grid=(last + 1,),
        in_specs=[
            stacked(d, 0),
            pl.BlockSpec((rows, d), whole),
            stacked(d, 1),
            pl.BlockSpec((gni_rows, wide), lambda i, s: (jnp.maximum(i - GN_BLOCKS - 1, 0), 0)),
            pl.BlockSpec((d, gn_cols), lambda i, s: (0, jnp.minimum(i, GN_BLOCKS - 1))),
            pl.BlockSpec(par.shape, whole),
            pl.BlockSpec(hp.shape, whole),
        ]
        + [any_spec] * 6,
        out_specs=[
            stacked(wide, 2),
            stacked(d, 2),
            stacked(d, 2),
            pl.BlockSpec((rows, d), whole),
            pl.BlockSpec((8, cw), whole),
        ],
        scratch_shapes=[
            pltpu.VMEM((rows, wide), F32),
            pltpu.VMEM((rows, cw), F32),
            pltpu.VMEM((rows, di), F32),
            pltpu.VMEM((rows, di), F32),
            pltpu.VMEM((rows, d), F32),
            pltpu.VMEM((2, rows, LANE), F32),
            pltpu.VMEM((pairs, 8, rows), F32),
            pltpu.VMEM((rows, LANE), F32),
            pltpu.VMEM((pairs, 8, rows), F32),
            pltpu.VMEM((rows, LANE), F32),
            pltpu.VMEM((rows, rows), F32),
            pltpu.VMEM((rows, rows), F32),
            pltpu.VMEM((rows, rows), F32),
            pltpu.VMEM((2, rows, LANE), F32),
            pltpu.SemaphoreType.DMA((4,)),
        ],
    )
    outs = pl.pallas_call(
        bwd_kernel,
        grid_spec=grid_spec,
        out_shape=[jax.ShapeDtypeStruct(v.shape, v.dtype) for v in held]
        + [jax.ShapeDtypeStruct((rows, d), BF16), jax.ShapeDtypeStruct((8, cw), F32)],
        input_output_aliases={11 + k: k for k in range(3)},
        compiler_params=pltpu.CompilerParams(vmem_limit_bytes=VMEM_LIMIT),
        cost_estimate=pl.CostEstimate(
            flops=2 * rows * d * (wide + di), bytes_accessed=60 << 20, transcendentals=4 << 20
        ),
        name="mixer_backward",
    )(scal, cot, recv, resid, w_in, w_out_t, par, hp, *kept, *held)
    return outs[:3], outs[3], outs[4]


def passed_along(shard, axis, by):
    length = lax.axis_size(axis)
    pairs = [(i, i + by) for i in range(length) if 0 <= i + by < length]
    return lax.ppermute(shard, axis, pairs)


def shards(
    x_in, lengths, norm_pre, w_in, conv_w, conv_b, dt_bias, a_log, skip_scale, norm_gate, w_out, cotangent
):
    section = lax.axis_index("section")
    micros, rows, d = x_in.shape
    heads = dt_bias.shape[1]
    taps = conv_w.shape[1]
    devices = lax.axis_size("dp")
    piece, wide = w_in.shape[1], w_in.shape[2]
    di = w_out.shape[1]
    cw_piece, gate_piece = conv_w.shape[2], norm_gate.shape[1]
    cw = cw_piece * devices
    pad = LANE - heads

    small = jnp.concatenate(
        [norm_pre[0], conv_b[0], norm_gate[0], conv_w[0].reshape(-1)]
    )
    small = jnp.pad(small, (0, piece * pad - small.shape[0])).reshape(piece, pad)
    gathered_in = lax.all_gather(jnp.concatenate([w_in[0], small], axis=1), "dp", axis=0, tiled=True)
    gathered_out = lax.all_gather(w_out[0].T, "dp", axis=0, tiled=True)
    tails = gathered_in[:, wide:].reshape(devices, piece * pad).astype(F32)
    ends = [0]
    for size in (piece, cw_piece, gate_piece, taps * cw_piece):
        ends.append(ends[-1] + size)
    gain_pre = tails[:, ends[0] : ends[1]].reshape(-1)
    conv_bias = tails[:, ends[1] : ends[2]].reshape(-1)
    gate_gain = tails[:, ends[2] : ends[3]].reshape(-1)
    conv_taps = tails[:, ends[3] : ends[4]].reshape(devices, taps, cw_piece)
    conv_taps = conv_taps.transpose(1, 0, 2).reshape(taps, cw)

    def wide_row(v):
        return jnp.pad(v, (0, cw - v.shape[0]))[None]

    par = jnp.concatenate(
        [
            conv_taps,
            conv_bias[None],
            wide_row(gate_gain),
            wide_row(jnp.repeat(skip_scale[0], di // heads)),
            wide_row(gain_pre),
        ],
        axis=0,
    )
    hp = jnp.pad(jnp.stack([dt_bias[0], -jnp.exp(a_log[0])]), ((0, 6), (0, pad)))

    first_end = lengths[:, 0, 0]
    second_end = first_end + lengths[:, 0, 1]
    slots = micros + 1

    def stack(width, dtype):
        return jnp.zeros((slots, rows, width), dtype)

    held = (
        stack(d, BF16), stack(di, BF16), stack(d, F32), stack(d, F32),
        stack(wide + pad, F32), stack(cw, F32), stack(di, F32),
    )
    recv = jnp.zeros((rows, d), BF16)
    stats = jnp.zeros((8, LANE), F32)
    valid_total = jnp.zeros((), F32)
    for step_no in range(micros + 1):
        micro = step_no - section
        live = (micro >= 0) & (micro < micros)
        clipped = jnp.clip(micro, 0, micros - 1)
        scal = jnp.stack(
            [clipped, jnp.where(live, clipped, micros), first_end[clipped], second_end[clipped]]
        ).astype(jnp.int32)
        held, branch, stat = forward_step(scal, x_in, recv, gathered_in, gathered_out, par, hp, held)
        stats = stats + jnp.where(live, stat, 0.0)
        valid_total = valid_total + jnp.where(live, second_end[clipped], 0).astype(F32)
        if step_no < micros:
            recv = passed_along(branch, "section", 1)
    normed_in, normed_out, outputs, resid, proj, csum, mixed = held

    back = (stack(wide + pad, BF16), stack(d, BF16), stack(d, F32))
    recv = jnp.zeros((rows, d), BF16)
    packs = None
    for step_no in range(micros + 1):
        micro = step_no - 1 + section
        live = (micro >= 0) & (micro < micros)
        clipped = jnp.clip(micro, 0, micros - 1)
        scal = jnp.stack(
            [
                clipped, clipped, jnp.where(live, clipped, micros),
                first_end[clipped], second_end[clipped], live & (section == 1),
            ]
        ).astype(jnp.int32)
        back, sent, pack = backward_step(
            scal, cotangent, recv, gathered_in, gathered_out, par, hp, resid, (proj, csum, mixed), back
        )
        packs = pack if packs is None else packs + pack
        if step_no < micros:
            recv = passed_along(sent, "section", -1)
    grad_proj, grad_branch, in_grad = back

    def joined(v):
        return v[:micros].reshape(micros * rows, v.shape[2])

    weight_out = dot_tn(joined(grad_branch), joined(normed_out)).astype(BF16)
    weight_in = dot_tn(joined(normed_in), joined(grad_proj)).astype(BF16)
    out_shard = lax.psum_scatter(weight_out, "dp", scatter_dimension=0, tiled=True).astype(F32).T
    in_shard = lax.psum_scatter(weight_in, "dp", scatter_dimension=0, tiled=True).astype(F32)[:, :wide]

    scalars = jnp.concatenate([stats[0, :2], valid_total[None]])
    packs, scalars = lax.psum((packs, scalars), "dp")
    me = lax.axis_index("dp")
    per_head = packs[6, :di].reshape(heads, di // heads).sum(axis=1)
    rms = jnp.sqrt(scalars[:2] / (scalars[2] * d))

    def mine(v, size):
        return lax.dynamic_slice_in_dim(v, me * size, size, axis=v.ndim - 1)

    return (
        outputs[:micros][None],
        in_grad[:micros][None],
        mine(packs[7, :d], piece)[None],
        in_shard[None],
        mine(packs[:taps], cw_piece)[None],
        mine(packs[4], cw_piece)[None],
        packs[7, d : d + heads][None],
        packs[7, d + LANE : d + LANE + heads][None],
        per_head[None],
        mine(packs[5, :di], gate_piece)[None],
        out_shard[None],
        rms[None],
    )


def solution(mesh):
    placed = (
        P(None, "dp", None),
        P(None, "dp", None),
        P("section", "dp"),
        P("section", "dp", None),
        P("section", None, "dp"),
        P("section", "dp"),
        P("section", None),
        P("section", None),
        P("section", None),
        P("section", "dp"),
        P("section", None, "dp"),
        P(None, "dp", None),
    )
    return jax.shard_map(
        shards,
        mesh=mesh,
        in_specs=placed,
        out_specs=(
            P("section", None, "dp", None),
            P("section", None, "dp", None),
            P("section", "dp"),
            P("section", "dp", None),
            P("section", None, "dp"),
            P("section", "dp"),
            P("section", None),
            P("section", None),
            P("section", None),
            P("section", "dp"),
            P("section", None, "dp"),
            P("section", None),
        ),
        check_vma=False,
    )
```

time: 1580 us -> 979 us (0.62)
  matrix products: 404 us -> 26.6 us
  Pallas kernels: 0 us -> 227 us
  other arithmetic: 247 us -> 21.4 us
  blocking collectives: 161 us -> 29.5 us
  local copies, waits for them, and re-layouts: 171 us -> 68.4 us
  waiting for transfers between devices: 540 us -> 572 us
  between operations: 33.9 us -> 17.2 us
    dot_general x38 -> x2, matrix products: 404 us -> 26.6 us  [dot_tn(): lax.dot_general(a, b, (((0,), (0,)), ((), ())), preferred_element_type=F3...]
    pallas_call x0 -> x6, Pallas kernels: none -> 227 us  [the longest x3 122 us: backward_step(): pl.pallas_call(bwd_kernel, grid_spec=grid_spec, out_shape=[jax.ShapeDtype...]
    all_gather x2, waiting for transfers between devices: 0.04 us -> 181 us  [the longest x1 100 us: shards(): lax.all_gather(jnp.concatenate([w_in[0], small], axis=1), 'dp', axis=0, t...]
    reduce_scatter x2, waiting for transfers between devices: 480 us -> 316 us  [the longest x1 206 us: shards(): lax.psum_scatter(weight_in, 'dp', scatter_dimension=0, tiled=True)]
    unnamed x2 -> x0, blocking collectives: 125 us -> none
    slice x28 -> x10, local copies, waits for them, and re-layouts: 114 us -> 5.64 us  [the longest x1 1.21 us: shards(): packs[7, d + LANE:d + LANE + heads][None]]
    reduce_sum x22 -> x1, other arithmetic: 85.1 us -> 0.63 us  [shards(): per_head = packs[6, :di].reshape(heads, di // heads).sum(axis=1)]
    another operation x32 -> x4, other arithmetic: 54.1 us -> 6.99 us  [the longest x3 5.73 us: shards(): jnp.stack([clipped, jnp.where(live, clipped, micros), first_end[clipped],...]
  transfers between devices with their start and end apart: 11 -> 9, of which waited for: 5 -> 9; matrix products, arithmetic and copies ran while one was open for 21% -> 7% of each run, Pallas kernels for 0% -> 0%
where the time goes in v1:
time: 979 us; the launch traced here: 973 us
  waiting for transfers between devices  572 us (58%)
  Pallas kernels  227 us (23%)
  local copies, waits for them, and re-layouts  68.4 us (7%)
  blocking collectives  29.5 us (3%)
  matrix products  26.6 us (3%)
  other arithmetic  21.4 us (2%)
  between operations  17.2 us (2%)
  starting transfers between devices  10.5 us (1%)
    reduce_scatter x1, waiting for transfers between devices, shards(): lax.psum_scatter(weight_in, 'dp', scatter_dimension=0, tiled=True)  206 us
    pallas_call x3, Pallas kernels, backward_step(): pl.pallas_call(bwd_kernel, grid_spec=grid_spec, out_shape=[jax.ShapeDtype...  122 us
    reduce_scatter x1, waiting for transfers between devices, shards(): lax.psum_scatter(weight_out, 'dp', scatter_dimension=0, tiled=True)  109 us
    pallas_call x3, Pallas kernels, forward_step(): pl.pallas_call(fwd_kernel, grid_spec=grid_spec, out_shape=[jax.ShapeDtype...  105 us
    all_gather x1, waiting for transfers between devices, shards(): lax.all_gather(jnp.concatenate([w_in[0], small], axis=1), 'dp', axis=0, t...  100 us
    all_gather x1, waiting for transfers between devices, shards(): gathered_out = lax.all_gather(w_out[0].T, 'dp', axis=0, tiled=True)  80.6 us
    ppermute x4, waiting for transfers between devices, passed_along(): return lax.ppermute(shard, axis, pairs)  61.2 us
    psum x1, blocking collectives, shards(): packs, scalars = lax.psum((packs, scalars), 'dp')  29.5 us
  transfers between devices with their start and end apart: 9, of which 9 were waited for; matrix products, arithmetic and copies ran while one was open for 7% of the time, Pallas kernels for 0%

profile of v1, /device:TPU:0, one launch (start us, length us, event | category | flops | bytes accessed | tf_op | source)
XLA Modules:
  0.0 972.9 jit_solution(17761009828780364542)
XLA Ops:
  10.3 2.4 pad_maximum_fusion
  19.7 100.4 %all-gather.3.cloned.1.call-done.win_ref = bf16[1536,6528]{1,0:T(8,128)(2,1)} async-done(((bf16[96,6528]{1,0:T(8,128)(2,1)}), bf16[1536,6528]{1,0:T(8,128)(2,1)}) %all-gather.3.cloned.1.call-update) | async-done | bytes 20054032 | tf_op jit(solution)/shard_map/all_gather | solution.py:521
  123.2 80.6 %all-gather.5.cloned.1.call-done.wout_ref = bf16[1536,3072]{1,0:T(8,128)(2,1)} async-done(((bf16[96,3072]{1,0:T(8,128)(2,1)}), bf16[1536,3072]{1,0:T(8,128)(2,1)}) %all-gather.5.cloned.1.call-update) | async-done | bytes 9437200 | tf_op jit(solution)/shard_map/all_gather | solution.py:522
  204.7 8.0 broadcast_in_dim.71.rest_4_
  212.8 4.5 broadcast_in_dim.72.rest_5_
  217.3 4.7 broadcast_in_dim.73.rest_6_
  222.0 2.7 broadcast_4_rest_2__rest_3__rest_5_.2.clone.rest_2_
  224.8 2.7 broadcast_4_rest_2__rest_3__rest_5_.2.clone.1.rest_3_
  227.5 2.7 broadcast_in_dim.70.rest_1_
  231.9 34.9 %mixer_forward.3 = (bf16[3,256,1536]{2,1,0:T(8,128)(2,1)}, bf16[3,256,3072]{2,1,0:T(8,128)(2,1)}, f32[3,256,1536]{2,1,0:T(8,128)}, f32[3,256,1536]{2,1,0:T(8,128...) custom-call(s32[4]{0:T(128)} %pad_add_fusion.2.scal, ...), custom_call_target="tpu_custom_call", output_to_operand_aliasing={{0}: (7, {}), {1}: (8, {}), {2}: (9, {}), {3}: (10, {}), {4... | custom-call | flops 7549747200 | bytes 62914560 | tf_op jit(solution)/shard_map/mixer_forward/pallas_call | solution.py:234
  266.7 3.4 collective-permute-start
  272.1 15.6 %collective-permute-done.recv_ref = bf16[256,1536]{1,0:T(8,128)(2,1)S(1)} collective-permute-done((bf16[256,1536]{1,0:T(8,128)(2,1)}, bf16[256,1536]{1,0:T(8,128)(2,1)S(1)}, u32[]{:S(2)}, u32[]{:S(2)}) %collective-permute-start) | collective-permute-done | bytes 786464 | tf_op jit(solution)/shard_map/ppermute | solution.py:500
  288.5 34.9 %mixer_forward.4 = (bf16[3,256,1536]{2,1,0:T(8,128)(2,1)}, bf16[3,256,3072]{2,1,0:T(8,128)(2,1)}, f32[3,256,1536]{2,1,0:T(8,128)}, f32[3,256,1536]{2,1,0:T(8,128...) custom-call(s32[4]{0:T(128)} %pad_add_fusion.1.scal, ...), custom_call_target="tpu_custom_call", output_to_operand_aliasing={{0}: (7, {}), {1}: (8, {}), {2}: (9, {}), {3}: (10, {}), {4... | custom-call | flops 7549747200 | bytes 62914560 | tf_op jit(solution)/shard_map/mixer_forward/pallas_call | solution.py:234
  323.5 4.3 collective-permute-start.1
  331.5 12.9 %collective-permute-done.1.recv_ref = bf16[256,1536]{1,0:T(8,128)(2,1)S(1)} collective-permute-done((bf16[256,1536]{1,0:T(8,128)(2,1)}, bf16[256,1536]{1,0:T(8,128)(2,1)S(1)}, u32[]{:S(2)}, u32[]{:S(2)}) %collective-permute-start.1) | collective-permute-done | bytes 786464 | tf_op jit(solution)/shard_map/ppermute | solution.py:500
  345.3 35.1 %mixer_forward.5 = (bf16[3,256,1536]{2,1,0:T(8,128)(2,1)}, bf16[3,256,3072]{2,1,0:T(8,128)(2,1)}, f32[3,256,1536]{2,1,0:T(8,128)}, f32[3,256,1536]{2,1,0:T(8,128...) custom-call(s32[4]{0:T(128)} %pad_add_fusion.scal, ...), custom_call_target="tpu_custom_call", output_to_operand_aliasing={{0}: (7, {}), {1}: (8, {}), {2}: (9, {}), {3}: (10, {}), {4... | custom-call | flops 7549747200 | bytes 62914560 | tf_op jit(solution)/shard_map/mixer_forward/pallas_call | solution.py:234
  380.4 4.5 broadcast_in_dim.75.rest_3_
  384.9 2.9 broadcast_4_rest_2__rest_3__rest_5_.2.rest_5_
  389.4 40.7 %mixer_backward.3 = (bf16[3,256,6528]{2,1,0:T(8,128)(2,1)}, bf16[3,256,1536]{2,1,0:T(8,128)(2,1)}, f32[3,256,1536]{2,1,0:T(8,128)}, bf16[256,1536]{1,0:T(8,128)(2,1)}, f32[8,3328]{1,0:T(8,128)}) custom-call(s32[6]{0:T(128)} %stack.103.scal, bf16[2,256,1536]{2,1,0:T(8,128)(2,1)} %cot_ref.5, ...), custom_call_target="tpu_custom_call", output_to_operand_aliasing={{0}: (11, {}), {1}: (12, {}), {2}: (13, {})} | custom-call | flops 7549747200 | bytes 62914560 | tf_op jit(solution)/shard_map/mixer_backward/pallas_call | solution.py:482
  433.4 16.8 %collective-permute-done.2.recv_ref = bf16[256,1536]{1,0:T(8,128)(2,1)S(1)} collective-permute-done((bf16[256,1536]{1,0:T(8,128)(2,1)}, bf16[256,1536]{1,0:T(8,128)(2,1)S(1)}, u32[]{:S(2)}, u32[]{:S(2)}) %collective-permute-start.2) | collective-permute-done | bytes 786464 | tf_op jit(solution)/shard_map/ppermute | solution.py:500
  451.1 40.7 %mixer_backward.4 = (bf16[3,256,6528]{2,1,0:T(8,128)(2,1)}, bf16[3,256,1536]{2,1,0:T(8,128)(2,1)}, f32[3,256,1536]{2,1,0:T(8,128)}, bf16[256,1536]{1,0:T(8,128)(2,1)}, f32[8,3328]{1,0:T(8,128)}) custom-call(s32[6]{0:T(128)} %stack.98.scal, bf16[2,256,1536]{2,1,0:T(8,128)(2,1)} %cot_ref.5, ...), custom_call_target="tpu_custom_call", output_to_operand_aliasing={{0}: (11, {}), {1}: (12, {}), {2}: (13, {})} | custom-call | flops 7549747200 | bytes 62914560 | tf_op jit(solution)/shard_map/mixer_backward/pallas_call | solution.py:482
  495.0 15.9 %collective-permute-done.3.recv_ref = bf16[256,1536]{1,0:T(8,128)(2,1)S(1)} collective-permute-done((bf16[256,1536]{1,0:T(8,128)(2,1)}, bf16[256,1536]{1,0:T(8,128)(2,1)S(1)}, u32[]{:S(2)}, u32[]{:S(2)}) %collective-permute-start.3) | collective-permute-done | bytes 786464 | tf_op jit(solution)/shard_map/ppermute | solution.py:500
  511.8 40.9 %mixer_backward.5 = (bf16[3,256,6528]{2,1,0:T(8,128)(2,1)}, bf16[3,256,1536]{2,1,0:T(8,128)(2,1)}, f32[3,256,1536]{2,1,0:T(8,128)}, bf16[256,1536]{1,0:T(8,128)(2,1)}, f32[8,3328]{1,0:T(8,128)}) custom-call(s32[6]{0:T(128)} %stack.93.scal, bf16[2,256,1536]{2,1,0:T(8,128)(2,1)} %cot_ref.5, ...), custom_call_target="tpu_custom_call", output_to_operand_aliasing={{0}: (11, {}), {1}: (12, {}), {2}: (13, {})} | custom-call | flops 7549747200 | bytes 62914560 | tf_op jit(solution)/shard_map/mixer_backward/pallas_call | solution.py:482
  554.4 9.4 bitcast_convert_fusion.1
  565.5 17.1 %bitcast_convert_fusion = bf16[1536,6528]{1,0:T(8,128)(2,1)} fusion(bf16[3,256,1536]{2,1,0:T(8,128)(2,1)S(1)} %copy-done, bf16[3,256,6528]{2,1,0:T(8,128)(2,1)} %get-tuple-element.86), kind=kOutput, calls=%fused_computation | convolution fusion | flops 10277683200 | bytes 29097984 | tf_op jit(solution)/shard_map/dot_general | solution.py:37
  584.8 29.5 %psum.15 = f32[3]{0:T(128)S(1)} all-reduce(f32[3]{0:T(128)S(1)} %pad_maximum_fusion.1), channel_id=1, replica_groups=mesh['section'=2,'dp'=16] {'dp'}, use_global_device_ids=true, to_apply=%region_4.5 | all-reduce | flops 3 | bytes 24 | tf_op jit(solution)/shard_map/psum | solution.py:606
  616.1 3.8 slice_bitcast_fusion.1
  619.8 3.8 slice_bitcast_fusion
  623.6 13.3 %all-reduce.7.cloned.1.call-done = f32[8,3328]{1,0:T(8,128)} async-done(((f32[8,3328]{1,0:T(8,128)}), f32[8,3328]{1,0:T(8,128)}) %all-reduce.7.cloned.1.call-update) | async-done | bytes 106512 | tf_op jit(solution)/shard_map/psum | solution.py:606
  644.9 109.4 %reduce-scatter.5.cloned.1.call-done = bf16[96,3072]{1,0:T(8,128)(2,1)} async-done(((bf16[1536,3072]{1,0:T(8,128)(2,1)}), bf16[96,3072]{1,0:T(8,128)(2,1)}) %reduce-scatter.5.cloned.1.call-update) | async-done | bytes 589840 | tf_op jit(solution)/shard_map/reduce_scatter | solution.py:602
  756.5 206.4 %reduce-scatter.3.cloned.1.call-done = bf16[96,6528]{1,0:T(8,128)(2,1)} async-done(((bf16[1536,6528]{1,0:T(8,128)(2,1)}), bf16[96,6528]{1,0:T(8,128)(2,1)}) %reduce-scatter.3.cloned.1.call-update) | async-done | bytes 1253392 | tf_op jit(solution)/shard_map/reduce_scatter | solution.py:603
  962.9 2.9 fusion.2
  (90 shorter events, 47.5 us)
Async XLA Ops:
  7.2 112.9 %all-gather.3.cloned.1.call-start = ((), (), s32[]{:S(2)}) async-start(), calls=%async_computation.2 | async-start | bytes 21307392 | tf_op jit(solution)/shard_map/all_gather | solution.py:521
  12.7 191.1 %all-gather.5.cloned.1.call-start = ((), (), s32[]{:S(2)}) async-start(), calls=%async_computation.3 | async-start | bytes 10027008 | tf_op jit(solution)/shard_map/all_gather | solution.py:522
  13.5 623.4 %all-reduce.7.cloned.1.call-start = ((), (), s32[]{:S(2)}) async-start(), calls=%async_computation.4 | async-start | bytes 212992 | tf_op jit(solution)/shard_map/psum | solution.py:606
  266.7 20.9 %collective-permute-start = (bf16[256,1536]{1,0:T(8,128)(2,1)}, bf16[256,1536]{1,0:T(8,128)(2,1)S(1)}, u32[]{:S(2)}, u32[]{:S(2)}) collective-permute-start(bf16[256,1536]{1,0:T(8,128)(2,1)} %get-tuple-element.52), channel_id=1, source_target_pairs={{0,16},{1,17},{2,18},{3,19},{4,20},{5,21},{6,22},{7,23},{8,24},{9,... | collective-permute-start | bytes 2359304 | tf_op jit(solution)/shard_map/ppermute | solution.py:500
  287.6 0.9 copy-start.2
  323.5 20.9 %collective-permute-start.1 = (bf16[256,1536]{1,0:T(8,128)(2,1)}, bf16[256,1536]{1,0:T(8,128)(2,1)S(1)}, u32[]{:S(2)}, u32[]{:S(2)}) collective-permute-start(bf16[256,1536]{1,0:T(8,128)(2,1)} %get-tuple-element.60), channel_id=1, source_target_pairs={{0,16},{1,17},{2,18},{3,19},{4,20},{5,21},{6,22},{7,23},{8,24},{9,... | collective-permute-start | bytes 2359304 | tf_op jit(solution)/shard_map/ppermute | solution.py:500
  344.4 0.9 copy-start.1
  430.1 20.1 %collective-permute-start.2 = (bf16[256,1536]{1,0:T(8,128)(2,1)}, bf16[256,1536]{1,0:T(8,128)(2,1)S(1)}, u32[]{:S(2)}, u32[]{:S(2)}) collective-permute-start(bf16[256,1536]{1,0:T(8,128)(2,1)} %get-tuple-element.73), channel_id=1, source_target_pairs={{16,0},{17,1},{18,2},{19,3},{20,4},{21,5},{22,6},{23,7},{24,8},{25... | collective-permute-start | bytes 2359304 | tf_op jit(solution)/shard_map/ppermute | solution.py:500
  450.2 0.9 copy-start.4
  491.8 19.1 %collective-permute-start.3 = (bf16[256,1536]{1,0:T(8,128)(2,1)}, bf16[256,1536]{1,0:T(8,128)(2,1)S(1)}, u32[]{:S(2)}, u32[]{:S(2)}) collective-permute-start(bf16[256,1536]{1,0:T(8,128)(2,1)} %get-tuple-element.77), channel_id=1, source_target_pairs={{16,0},{17,1},{18,2},{19,3},{20,4},{21,5},{22,6},{23,7},{24,8},{25... | collective-permute-start | bytes 2359304 | tf_op jit(solution)/shard_map/ppermute | solution.py:500
  510.9 0.9 copy-start.3
  511.8 40.9 %copy-start.5 = (f32[8,3328]{1,0:T(8,128)S(1)}, f32[8,3328]{1,0:T(8,128)}, u32[]{:S(2)}) copy-start(f32[8,3328]{1,0:T(8,128)} %get-tuple-element.82) | copy-start | bytes 319492
  511.8 40.9 %copy-start.6 = (f32[8,3328]{1,0:T(8,128)S(1)}, f32[8,3328]{1,0:T(8,128)}, u32[]{:S(2)}) copy-start(f32[8,3328]{1,0:T(8,128)} %get-tuple-element.83) | copy-start | bytes 319492
  554.4 200.0 %reduce-scatter.5.cloned.1.call-start = ((), (), s32[]{:S(2)}) async-start(), calls=%async_computation.6 | async-start | bytes 10027008 | tf_op jit(solution)/shard_map/reduce_scatter | solution.py:602
  563.8 1.7 copy-start
  563.9 399.0 %reduce-scatter.3.cloned.1.call-start = ((), (), s32[]{:S(2)}) async-start(), calls=%async_computation.5 | async-start | bytes 21307392 | tf_op jit(solution)/shard_map/reduce_scatter | solution.py:603
  582.7 2.0 copy-start.7
  582.7 2.0 copy-start.8
  582.7 2.0 copy-start.9
Sparse Core Ops, SparseCore 0:
  12.8 107.2 all-gather.2
  122.4 81.4 all-gather.4
  554.5 82.3 all-reduce.6
  640.8 113.5 reduce-scatter.4
  759.0 203.8 reduce-scatter.2

commit v2 on v1

--- a/solution.py
+++ b/solution.py
@@ -81,9 +81,8 @@
 def fwd_kernel(
     scal, x_ref, recv_ref, win_ref, wout_ref, par_ref, hp_ref, *rest
 ):
-    (a0, a1, a2, a3, a4, a5, a6,
-     nin_ref, nout_ref, out_ref, resid_ref, proj_hbm, csum_hbm, mixed_hbm, branch_ref, stat_ref,
-     proj, csum, act, mixed, gated, ld_s, lr_t, cb, maskb, sem) = rest
+    (nin_ref, nout_ref, out_ref, resid_ref, proj_hbm, csum_hbm, mixed_hbm, branch_ref, stat_ref,
+     proj, csum, act, mixed, gated, ld_s, lr_t, cb, maskb, sem) = rest[-19:]
     step = pl.program_id(0)
     rows, di, cw = gated.shape[0], gated.shape[1], csum.shape[1]
     half = rows // 2
@@ -190,7 +189,7 @@
             copy.wait()
 
 
-def forward_step(scal, x_in, recv, w_in, w_out_t, par, hp, held):
+def forward_step(scal, x_in, recv, w_in, w_out_t, par, hp, stacks, held):
     rows, d = recv.shape
     di = w_out_t.shape[1]
     wide = w_in.shape[1]
@@ -214,7 +213,7 @@
             pl.BlockSpec(par.shape, whole),
             pl.BlockSpec(hp.shape, whole),
         ]
-        + [any_spec] * 7,
+        + [any_spec] * len(held),
         out_specs=[stacked(d), stacked(di), stacked(d), stacked(d)]
         + [any_spec] * 3
         + [pl.BlockSpec((rows, d), whole), pl.BlockSpec((8, LANE), whole)],
@@ -234,9 +233,9 @@
     outs = pl.pallas_call(
         fwd_kernel,
         grid_spec=grid_spec,
-        out_shape=[jax.ShapeDtypeStruct(v.shape, v.dtype) for v in held]
+        out_shape=list(stacks)
         + [jax.ShapeDtypeStruct((rows, d), BF16), jax.ShapeDtypeStruct((8, LANE), F32)],
-        input_output_aliases={7 + k: k for k in range(7)},
+        input_output_aliases={7 + k: k for k in range(len(held))},
         compiler_params=pltpu.CompilerParams(vmem_limit_bytes=VMEM_LIMIT),
         cost_estimate=pl.CostEstimate(
             flops=2 * rows * d * (wide + di), bytes_accessed=60 << 20, transcendentals=4 << 20
@@ -247,9 +246,9 @@
 
 
 def bwd_kernel(scal, cot_ref, recv_ref, resid_ref, win_ref, wout_ref, par_ref, hp_ref, *rest):
-    (proj_hbm, csum_hbm, mixed_hbm, a0, a1, a2,
-     gproj_ref, gbr_ref, ing_ref, send_ref, pack_ref,
-     proj, csum, mixed, gn, gni, act_bc, ld_t, lr_s, row_q, col_q, cbt, dcbt, maskb, stat, sem) = rest
+    proj_hbm, csum_hbm, mixed_hbm = rest[:3]
+    (gproj_ref, gbr_ref, ing_ref, send_ref, pack_ref,
+     proj, csum, mixed, gn, gni, act_bc, ld_t, lr_s, row_q, col_q, cbt, dcbt, maskb, stat, sem) = rest[-20:]
     step = pl.program_id(0)
     rows, di, cw = mixed.shape[0], mixed.shape[1], csum.shape[1]
     d = gni.shape[1]
@@ -427,7 +426,7 @@
         pack_ref[7:8, :d] = col_sum(u * q * gi)
 
 
-def backward_step(scal, cot, recv, w_in, w_out_t, par, hp, resid, kept, held):
+def backward_step(scal, cot, recv, w_in, w_out_t, par, hp, resid, kept, stacks, held):
     rows, d = recv.shape
     di = w_out_t.shape[1]
     wide = w_in.shape[1]
@@ -453,7 +452,7 @@
             pl.BlockSpec(par.shape, whole),
             pl.BlockSpec(hp.shape, whole),
         ]
-        + [any_spec] * 6,
+        + [any_spec] * (3 + len(held)),
         out_specs=[
             stacked(wide, 2),
             stacked(d, 2),
@@ -482,9 +481,9 @@
     outs = pl.pallas_call(
         bwd_kernel,
         grid_spec=grid_spec,
-        out_shape=[jax.ShapeDtypeStruct(v.shape, v.dtype) for v in held]
+        out_shape=list(stacks)
         + [jax.ShapeDtypeStruct((rows, d), BF16), jax.ShapeDtypeStruct((8, cw), F32)],
-        input_output_aliases={11 + k: k for k in range(3)},
+        input_output_aliases={11 + k: k for k in range(len(held))},
         compiler_params=pltpu.CompilerParams(vmem_limit_bytes=VMEM_LIMIT),
         cost_estimate=pl.CostEstimate(
             flops=2 * rows * d * (wide + di), bytes_accessed=60 << 20, transcendentals=4 << 20
@@ -492,6 +491,201 @@
         name="mixer_backward",
     )(scal, cot, recv, resid, w_in, w_out_t, par, hp, *kept, *held)
     return outs[:3], outs[3], outs[4]
+
+
+def ring_place(index, n):
+    chip, core = index // 2, index % 2
+    z, x = chip // 2, chip % 2
+    return 2 * ((1 - x) * z + x * (n // 2 - 1 - z)) + core
+
+
+def ring_device(place, n):
+    spot, core = place // 2, place % 2
+    far = spot // (n // 4)
+    chip = (1 - far) * (2 * spot) + far * (2 * (n // 2 - 1 - spot) + 1)
+    return 2 * chip + core
+
+
+def tile_chunks(columns, parts):
+    tiles = columns // LANE
+    cuts = [LANE * (-(-tiles * i // parts)) for i in range(parts + 1)]
+    return [(cuts[i], cuts[i + 1] - cuts[i]) for i in range(parts)]
+
+
+def greet_all(n, me, section):
+    barrier = pltpu.get_barrier_semaphore()
+
+    def signal(i, carry):
+        pl.semaphore_signal(
+            barrier, inc=1, device_id=(section, (me + i) % n), device_id_type=pl.DeviceIdType.MESH
+        )
+        return carry
+
+    lax.fori_loop(1, n, signal, 0)
+    pl.semaphore_wait(barrier, n - 1)
+
+
+def scatter_kernel(
+    n, nin_t, gbr_t, gproj_hbm, nout_hbm, small_ref,
+    gin_ref, gout_ref, small_out,
+    gproj, nout, held, small_got, load_sem, send_sem, recv_sem, small_send, small_recv,
+):
+    me = lax.axis_index("dp")
+    section = lax.axis_index("section")
+    place = ring_place(me, n)
+    steps = n // 2
+    micros, rows = gproj_hbm.shape[0] - 1, gproj_hbm.shape[1]
+    wide, di = gproj.shape[1], nout.shape[1]
+    targets = (ring_device((place + 1) % n, n), ring_device((place + n - 1) % n, n))
+    loads = []
+    for m in range(micros):
+        part = pl.ds(m * rows, rows)
+        loads.append(pltpu.make_async_copy(nout_hbm.at[m], nout.at[part], load_sem.at[0, m]))
+        loads.append(pltpu.make_async_copy(gproj_hbm.at[m], gproj.at[part], load_sem.at[1, m]))
+    for load in loads:
+        load.start()
+    greet_all(n, me, section)
+
+    def small_copy(other, slot):
+        return pltpu.make_async_remote_copy(
+            src_ref=small_ref.at[other],
+            dst_ref=small_got.at[slot],
+            send_sem=small_send.at[slot],
+            recv_sem=small_recv.at[slot],
+            device_id=(section, other),
+            device_id_type=pl.DeviceIdType.MESH,
+        )
+
+    def small_start(i, carry):
+        small_copy((me + i) % n, i).start()
+        return carry
+
+    lax.fori_loop(1, n, small_start, 0)
+    for load in loads:
+        load.wait()
+
+    out_cuts = tile_chunks(di, 2)
+    in_cuts = tile_chunks(wide, 4)
+    chunks = [
+        (False, *out_cuts[0]), (False, *out_cuts[1]),
+        (True, *in_cuts[0]), (True, *in_cuts[2]), (True, *in_cuts[1]), (True, *in_cuts[3]),
+    ]
+
+    def own(owner, chunk):
+        is_in, start, size = chunk
+        if is_in:
+            return dot_nn(nin_t[owner], gproj[:, start : start + size])
+        return dot_nn(gbr_t[owner], nout[:, start : start + size])
+
+    def columns(chunk):
+        is_in, start, size = chunk
+        return pl.ds(start if is_in else wide + start, size)
+
+    def owner_of(way, k):
+        shift = steps - k if way == 0 else n - steps + k
+        return ring_device((place + shift) % n, n)
+
+    def send(way, k, c):
+        cols = columns(chunks[c])
+        return pltpu.make_async_remote_copy(
+            src_ref=held.at[way, k, :, cols],
+            dst_ref=held.at[way, k + 1, :, cols],
+            send_sem=send_sem.at[way, k, c],
+            recv_sem=recv_sem.at[way, k, c],
+            device_id=(section, targets[way]),
+            device_id_type=pl.DeviceIdType.MESH,
+        )
+
+    def run_step(k, first, second):
+        for c, chunk in enumerate(chunks):
+            for way in range(2):
+                if first and c % 2 != way:
+                    continue
+                cols = columns(chunk)
+                total = own(owner_of(way, k), chunk)
+                if not first and not (second and c % 2 != way):
+                    send(way, k - 1, c).wait_recv()
+                    total += held[way, k, :, cols].astype(F32)
+                held[way, k, :, cols] = total.astype(BF16)
+                send(way, k, c).start()
+
+    run_step(0, True, False)
+    run_step(1, False, True)
+
+    def loop(k, carry):
+        run_step(k, False, False)
+        return carry
+
+    lax.fori_loop(2, steps, loop, 0)
+
+    for c, chunk in enumerate(chunks):
+        is_in, start, size = chunk
+        cols = columns(chunk)
+        total = own(me, chunk)
+        for way in range(2):
+            send(way, steps - 1, c).wait_recv()
+            total += held[way, steps, :, cols].astype(F32)
+        if is_in:
+            gin_ref[:, start : start + size] = total
+        else:
+            gout_ref[:, start : start + size] = total
+
+    small_out[...] = small_ref[me]
+
+    def small_end(i, carry):
+        copy = small_copy((me + i) % n, i)
+        copy.wait()
+        small_out[...] += small_got[i]
+        return carry
+
+    lax.fori_loop(1, n, small_end, 0)
+    for c in range(len(chunks)):
+        send(c % 2, 0, c).wait_send()
+
+    def sent(k, carry):
+        for c in range(len(chunks)):
+            for way in range(2):
+                send(way, k, c).wait_send()
+        return carry
+
+    lax.fori_loop(1, steps, sent, 0)
+
+
+def scatter_gradients(n, nin_t, gbr_t, gproj, nout, small):
+    piece, tokens = nin_t.shape[1:]
+    wide, di = gproj.shape[2], nout.shape[2]
+    micros = nout.shape[0] - 1
+    steps = n // 2
+    vmem = pl.BlockSpec(memory_space=pltpu.VMEM)
+    hbm = pl.BlockSpec(memory_space=pl.ANY)
+    return pl.pallas_call(
+        functools.partial(scatter_kernel, n),
+        out_shape=[
+            jax.ShapeDtypeStruct((piece, wide), F32),
+            jax.ShapeDtypeStruct((piece, di), F32),
+            jax.ShapeDtypeStruct(small.shape[1:], F32),
+        ],
+        in_specs=[vmem, vmem, hbm, hbm, vmem],
+        out_specs=[vmem, vmem, vmem],
+        scratch_shapes=[
+            pltpu.VMEM((tokens, wide), BF16),
+            pltpu.VMEM((tokens, di), BF16),
+            pltpu.VMEM((2, steps + 1, piece, wide + di), BF16),
+            pltpu.VMEM(small.shape, F32),
+            pltpu.SemaphoreType.DMA((2, micros)),
+            pltpu.SemaphoreType.DMA((2, steps, 6)),
+            pltpu.SemaphoreType.DMA((2, steps, 6)),
+            pltpu.SemaphoreType.DMA((n,)),
+            pltpu.SemaphoreType.DMA((n,)),
+        ],
+        compiler_params=pltpu.CompilerParams(
+            collective_id=0, has_side_effects=True, vmem_limit_bytes=VMEM_LIMIT
+        ),
+        cost_estimate=pl.CostEstimate(
+            flops=2 * n * piece * tokens * (wide + di), bytes_accessed=20 << 20, transcendentals=0
+        ),
+        name="gradient_scatter",
+    )(nin_t, gbr_t, gproj, nout, small)
 
 
 def passed_along(shard, axis, by):
@@ -550,12 +744,13 @@
     slots = micros + 1
 
     def stack(width, dtype):
-        return jnp.zeros((slots, rows, width), dtype)
-
-    held = (
+        return jax.ShapeDtypeStruct((slots, rows, width), dtype)
+
+    stacks = (
         stack(d, BF16), stack(di, BF16), stack(d, F32), stack(d, F32),
         stack(wide + pad, F32), stack(cw, F32), stack(di, F32),
     )
+    held = ()
     recv = jnp.zeros((rows, d), BF16)
     stats = jnp.zeros((8, LANE), F32)
     valid_total = jnp.zeros((), F32)
@@ -566,14 +761,15 @@
         scal = jnp.stack(
             [clipped, jnp.where(live, clipped, micros), first_end[clipped], second_end[clipped]]
         ).astype(jnp.int32)
-        held, branch, stat = forward_step(scal, x_in, recv, gathered_in, gathered_out, par, hp, held)
+        held, branch, stat = forward_step(scal, x_in, recv, gathered_in, gathered_out, par, hp, stacks, held)
         stats = stats + jnp.where(live, stat, 0.0)
         valid_total = valid_total + jnp.where(live, second_end[clipped], 0).astype(F32)
         if step_no < micros:
             recv = passed_along(branch, "section", 1)
     normed_in, normed_out, outputs, resid, proj, csum, mixed = held
 
-    back = (stack(wide + pad, BF16), stack(d, BF16), stack(d, F32))
+    stacks = (stack(wide + pad, BF16), stack(d, BF16), stack(d, F32))
+    back = ()
     recv = jnp.zeros((rows, d), BF16)
     packs = None
     for step_no in range(micros + 1):
@@ -587,42 +783,64 @@
             ]
         ).astype(jnp.int32)
         back, sent, pack = backward_step(
-            scal, cotangent, recv, gathered_in, gathered_out, par, hp, resid, (proj, csum, mixed), back
+            scal, cotangent, recv, gathered_in, gathered_out, par, hp, resid, (proj, csum, mixed), stacks, back
         )
         packs = pack if packs is None else packs + pack
         if step_no < micros:
             recv = passed_along(sent, "section", -1)
     grad_proj, grad_branch, in_grad = back
 
-    def joined(v):
-        return v[:micros].reshape(micros * rows, v.shape[2])
-
-    weight_out = dot_tn(joined(grad_branch), joined(normed_out)).astype(BF16)
-    weight_in = dot_tn(joined(normed_in), joined(grad_proj)).astype(BF16)
-    out_shard = lax.psum_scatter(weight_out, "dp", scatter_dimension=0, tiled=True).astype(F32).T
-    in_shard = lax.psum_scatter(weight_in, "dp", scatter_dimension=0, tiled=True).astype(F32)[:, :wide]
-
-    scalars = jnp.concatenate([stats[0, :2], valid_total[None]])
-    packs, scalars = lax.psum((packs, scalars), "dp")
+    def turned(v):
+        return v[:micros].reshape(micros * rows, d).T.reshape(devices, piece, micros * rows)
+
     me = lax.axis_index("dp")
     per_head = packs[6, :di].reshape(heads, di // heads).sum(axis=1)
-    rms = jnp.sqrt(scalars[:2] / (scalars[2] * d))
-
-    def mine(v, size):
-        return lax.dynamic_slice_in_dim(v, me * size, size, axis=v.ndim - 1)
+    common = jnp.concatenate(
+        [
+            packs[7, d : d + heads],
+            packs[7, d + LANE : d + LANE + heads],
+            per_head,
+            stats[0, :2],
+            valid_total[None],
+        ]
+    )
+    small = jnp.concatenate(
+        [
+            packs[:taps].reshape(taps, devices, cw_piece).transpose(1, 0, 2).reshape(devices, -1),
+            packs[4].reshape(devices, cw_piece),
+            packs[5, :di].reshape(devices, gate_piece),
+            packs[7, :d].reshape(devices, piece),
+            jnp.broadcast_to(common, (devices, common.shape[0])),
+        ],
+        axis=1,
+    )
+    small_rows = -(-small.shape[1] // (8 * LANE)) * 8
+    small = jnp.pad(small, ((0, 0), (0, small_rows * LANE - small.shape[1])))
+    in_shard, out_shard, small = scatter_gradients(
+        devices, turned(normed_in), turned(grad_branch), grad_proj, normed_out,
+        small.reshape(devices, small_rows, LANE),
+    )
+    small = small.reshape(-1)
+    parts = []
+    start = 0
+    for size in (taps * cw_piece, cw_piece, gate_piece, piece, heads, heads, heads, 3):
+        parts.append(small[start : start + size])
+        start += size
+    sums = parts[7]
+    rms = jnp.sqrt(sums[:2] / (sums[2] * d))
 
     return (
         outputs[:micros][None],
         in_grad[:micros][None],
-        mine(packs[7, :d], piece)[None],
-        in_shard[None],
-        mine(packs[:taps], cw_piece)[None],
-        mine(packs[4], cw_piece)[None],
-        packs[7, d : d + heads][None],
-        packs[7, d + LANE : d + LANE + heads][None],
-        per_head[None],
-        mine(packs[5, :di], gate_piece)[None],
-        out_shard[None],
+        parts[3][None],
+        in_shard[None, :, :wide],
+        parts[0].reshape(1, taps, cw_piece),
+        parts[1][None],
+        parts[4][None],
+        parts[5][None],
+        parts[6][None],
+        parts[2][None],
+        out_shard.T[None],
         rms[None],
     )
 

time: 979 us -> 715 us (0.73)
  waiting for transfers between devices: 572 us -> 236 us
  Pallas kernels: 227 us -> 387 us
  blocking collectives: 29.5 us -> 0 us
  local copies, waits for them, and re-layouts: 68.4 us -> 41.4 us
  matrix products: 26.6 us -> 0 us
    reduce_scatter x2 -> x0, waiting for transfers between devices: 316 us -> none  [the longest x1 206 us: shards(): lax.psum_scatter(weight_in, 'dp', scatter_dimension=0, tiled=True)]
    pallas_call x6 -> x7, Pallas kernels: 227 us -> 387 us  [the longest x1 160 us: scatter_gradients(): pl.pallas_call(functools.partial(scatter_kernel, n), out_shape=[jax.Shape...]
    psum x1 -> x0, blocking collectives: 29.5 us -> none  [shards(): packs, scalars = lax.psum((packs, scalars), 'dp')]
    dot_general x2 -> x0, matrix products: 26.6 us -> none  [dot_tn(): lax.dot_general(a, b, (((0,), (0,)), ((), ())), preferred_element_type=F3...]
    broadcast_in_dim x6 -> x4, local copies, waits for them, and re-layouts: 25.2 us -> 4.25 us  [the longest x1 1.62 us: shards(): in_shard[None, :, :wide]]
    psum x1 -> x0, waiting for transfers between devices: 13.3 us -> none  [shards(): packs, scalars = lax.psum((packs, scalars), 'dp')]
    another operation x6 -> x4, local copies, waits for them, and re-layouts: 12.5 us -> 1.15 us
    ppermute x4, waiting for transfers between devices: 61.2 us -> 51.4 us  [passed_along(): return lax.ppermute(shard, axis, pairs)]
  transfers between devices with their start and end apart: 9 -> 6, of which waited for: 9 -> 6; matrix products, arithmetic and copies ran while one was open for 7% -> 3% of each run, Pallas kernels for 0% -> 0%
where the time goes in v2:
time: 715 us; the launch traced here: 706 us
  Pallas kernels  387 us (54%)
  waiting for transfers between devices  236 us (33%)
  local copies, waits for them, and re-layouts  41.4 us (6%)
  between operations  17.6 us (2%)
  other arithmetic  13.6 us (2%)
  starting transfers between devices  10.9 us (2%)
    pallas_call x1, Pallas kernels, scatter_gradients(): pl.pallas_call(functools.partial(scatter_kernel, n), out_shape=[jax.Shape...  160 us
    pallas_call x3, Pallas kernels, backward_step(): pl.pallas_call(bwd_kernel, grid_spec=grid_spec, out_shape=list(stacks) +...  123 us
    pallas_call x3, Pallas kernels, forward_step(): pl.pallas_call(fwd_kernel, grid_spec=grid_spec, out_shape=list(stacks) +...  104 us
    all_gather x1, waiting for transfers between devices, shards(): lax.all_gather(jnp.concatenate([w_in[0], small], axis=1), 'dp', axis=0, t...  103 us
    all_gather x1, waiting for transfers between devices, shards(): gathered_out = lax.all_gather(w_out[0].T, 'dp', axis=0, tiled=True)  80.6 us
    ppermute x4, waiting for transfers between devices, passed_along(): return lax.ppermute(shard, axis, pairs)  51.4 us
  transfers between devices with their start and end apart: 6, of which 6 were waited for; matrix products, arithmetic and copies ran while one was open for 3% of the time, Pallas kernels for 0%

profile of v2, /device:TPU:0, one launch (start us, length us, event | category | flops | bytes accessed | tf_op | source)
XLA Modules:
  0.0 705.9 jit_solution(2792761583290887634)
XLA Ops:
  10.3 2.4 pad_maximum_fusion
  14.4 1.9 pad_add_fusion.2.scal
  16.9 103.2 %all-gather.3.cloned.1.call-done.win_ref = bf16[1536,6528]{1,0:T(8,128)(2,1)} async-done(((bf16[96,6528]{1,0:T(8,128)(2,1)}), bf16[1536,6528]{1,0:T(8,128)(2,1)}) %all-gather.3.cloned.1.call-update) | async-done | bytes 20054032 | tf_op jit(solution)/shard_map/all_gather | solution.py:715
  123.2 80.6 %all-gather.5.cloned.1.call-done.wout_ref = bf16[1536,3072]{1,0:T(8,128)(2,1)} async-done(((bf16[96,3072]{1,0:T(8,128)(2,1)}), bf16[1536,3072]{1,0:T(8,128)(2,1)}) %all-gather.5.cloned.1.call-update) | async-done | bytes 9437200 | tf_op jit(solution)/shard_map/all_gather | solution.py:716
  204.8 34.6 %mixer_forward.3 = (bf16[3,256,1536]{2,1,0:T(8,128)(2,1)}, bf16[3,256,3072]{2,1,0:T(8,128)(2,1)}, f32[3,256,1536]{2,1,0:T(8,128)}, f32[3,256,1536]{2,1,0:T(8,128...) custom-call(s32[4]{0:T(128)} %pad_add_fusion.2.scal, ...), custom_call_target="tpu_custom_call" | custom-call | flops 7549747200 | bytes 62914560 | tf_op jit(solution)/shard_map/mixer_forward/pallas_call | solution.py:233
  239.4 3.6 collective-permute-start
  243.0 1.8 pad_add_fusion.1.scal
  244.9 15.4 %collective-permute-done.recv_ref = bf16[256,1536]{1,0:T(8,128)(2,1)S(1)} collective-permute-done((bf16[256,1536]{1,0:T(8,128)(2,1)}, bf16[256,1536]{1,0:T(8,128)(2,1)S(1)}, u32[]{:S(2)}, u32[]{:S(2)}) %collective-permute-start) | collective-permute-done | bytes 786464 | tf_op jit(solution)/shard_map/ppermute | solution.py:694
  261.2 34.6 %mixer_forward.4 = (bf16[3,256,1536]{2,1,0:T(8,128)(2,1)}, bf16[3,256,3072]{2,1,0:T(8,128)(2,1)}, f32[3,256,1536]{2,1,0:T(8,128)}, f32[3,256,1536]{2,1,0:T(8,128...) custom-call(s32[4]{0:T(128)} %pad_add_fusion.1.scal, ...), custom_call_target="tpu_custom_call", output_to_operand_aliasing={{0}: (7, {}), {1}: (8, {}), {2}: (9, {}), {3}: (10, {}), {4... | custom-call | flops 7549747200 | bytes 62914560 | tf_op jit(solution)/shard_map/mixer_forward/pallas_call | solution.py:233
  295.8 4.6 collective-permute-start.1
  300.4 1.9 stack.103.scal
  302.3 1.9 pad_add_fusion.scal
  304.2 12.6 %collective-permute-done.1.recv_ref = bf16[256,1536]{1,0:T(8,128)(2,1)S(1)} collective-permute-done((bf16[256,1536]{1,0:T(8,128)(2,1)}, bf16[256,1536]{1,0:T(8,128)(2,1)S(1)}, u32[]{:S(2)}, u32[]{:S(2)}) %collective-permute-start.1) | collective-permute-done | bytes 786464 | tf_op jit(solution)/shard_map/ppermute | solution.py:694
  317.7 34.6 %mixer_forward.5 = (bf16[3,256,1536]{2,1,0:T(8,128)(2,1)}, bf16[3,256,3072]{2,1,0:T(8,128)(2,1)}, f32[3,256,1536]{2,1,0:T(8,128)}, f32[3,256,1536]{2,1,0:T(8,128...) custom-call(s32[4]{0:T(128)} %pad_add_fusion.scal, ...), custom_call_target="tpu_custom_call", output_to_operand_aliasing={{0}: (7, {}), {1}: (8, {}), {2}: (9, {}), {3}: (10, {}), {4... | custom-call | flops 7549747200 | bytes 62914560 | tf_op jit(solution)/shard_map/mixer_forward/pallas_call | solution.py:233
  352.3 41.1 %mixer_backward.3 = (bf16[3,256,6528]{2,1,0:T(8,128)(2,1)}, bf16[3,256,1536]{2,1,0:T(8,128)(2,1)}, f32[3,256,1536]{2,1,0:T(8,128)}, bf16[256,1536]{1,0:T(8,128)(2,1)}, f32[8,3328]{1,0:T(8,128)}) custom-call(s32[6]{0:T(128)} %stack.103.scal, bf16[2,256,1536]{2,1,0:T(8,128)(2,1)} %cot_ref.5, bf16[256,1536]{1,0:T(8,128)(2,1)} %broadcast_1_recv_ref.2.recv_ref, ...), custom_call_target="tpu_custom_call" | custom-call | flops 7549747200 | bytes 62914560 | tf_op jit(solution)/shard_map/mixer_backward/pallas_call | solution.py:481
  393.4 1.3 collective-permute-start.2
  396.7 1.9 stack.98.scal
  398.6 1.9 stack.93.scal
  401.7 2.7 copy.49
  404.5 9.1 %collective-permute-done.2.recv_ref = bf16[256,1536]{1,0:T(8,128)(2,1)S(1)} collective-permute-done((bf16[256,1536]{1,0:T(8,128)(2,1)}, bf16[256,1536]{1,0:T(8,128)(2,1)S(1)}, u32[]{:S(2)}, u32[]{:S(2)}) %collective-permute-start.2) | collective-permute-done | bytes 786464 | tf_op jit(solution)/shard_map/ppermute | solution.py:694
  414.4 40.6 %mixer_backward.4 = (bf16[3,256,6528]{2,1,0:T(8,128)(2,1)}, bf16[3,256,1536]{2,1,0:T(8,128)(2,1)}, f32[3,256,1536]{2,1,0:T(8,128)}, bf16[256,1536]{1,0:T(8,128)(2,1)}, f32[8,3328]{1,0:T(8,128)}) custom-call(s32[6]{0:T(128)} %stack.98.scal, bf16[2,256,1536]{2,1,0:T(8,128)(2,1)} %cot_ref.5, ...), custom_call_target="tpu_custom_call", output_to_operand_aliasing={{0}: (11, {}), {1}: (12, {}), {2}: (13, {})} | custom-call | flops 7549747200 | bytes 62914560 | tf_op jit(solution)/shard_map/mixer_backward/pallas_call | solution.py:481
  456.4 3.8 slice_bitcast_fusion.1
  460.1 14.2 %collective-permute-done.3.recv_ref = bf16[256,1536]{1,0:T(8,128)(2,1)S(1)} collective-permute-done((bf16[256,1536]{1,0:T(8,128)(2,1)}, bf16[256,1536]{1,0:T(8,128)(2,1)S(1)}, u32[]{:S(2)}, u32[]{:S(2)}) %collective-permute-start.3) | collective-permute-done | bytes 786464 | tf_op jit(solution)/shard_map/ppermute | solution.py:694
  475.2 40.8 %mixer_backward.5 = (bf16[3,256,6528]{2,1,0:T(8,128)(2,1)}, bf16[3,256,1536]{2,1,0:T(8,128)(2,1)}, f32[3,256,1536]{2,1,0:T(8,128)}, bf16[256,1536]{1,0:T(8,128)(2,1)}, f32[8,3328]{1,0:T(8,128)}) custom-call(s32[6]{0:T(128)} %stack.93.scal, bf16[2,256,1536]{2,1,0:T(8,128)(2,1)} %cot_ref.5, ...), custom_call_target="tpu_custom_call", output_to_operand_aliasing={{0}: (11, {}), {1}: (12, {}), {2}: (13, {})} | custom-call | flops 7549747200 | bytes 62914560 | tf_op jit(solution)/shard_map/mixer_backward/pallas_call | solution.py:481
  518.8 1.5 slice.100
  520.3 1.6 copy.50
  521.9 160.2 %gradient_scatter.1 = (f32[96,6528]{1,0:T(8,128)}, f32[96,3072]{1,0:T(8,128)}, f32[16,128]{1,0:T(8,128)}) custom-call(bf16[16,96,512]{2,1,0:T(8,128)(2,1)} %bitcast.83, bf16[16,96,512]{2,1,0:T(8,128)(2,1)} %bitcast.84, bf16[3,256,6528]{2,1,0:T(8,128)(2,1)} %get-tuple-element.87.gproj_hbm, bf16[3,256,3072]{2,1,0:T(8,128)(2,1)} %get-tuple-element.88.nout_hbm, ...), custom_call_target="tpu_custom_call" | custom-call | flops 15099494400 | bytes 20971520 | tf_op jit(solution)/shard_map/gradient_scatter/pallas_call | solution.py:661
  684.6 1.3 slice.137
  685.9 1.3 slice.133
  687.3 1.4 slice_bitcast_fusion.3
  689.3 3.9 slice_bitcast_fusion
  695.8 1.6 slice_bitcast_fusion.2
  (97 shorter events, 24.2 us)
Async XLA Ops:
  7.2 6.3 copy-start.13
  7.2 6.5 copy-start.9
  7.2 9.1 %copy-start.15 = (f32[1,48]{1,0:T(1,128)S(1)}, f32[1,48]{1,0:T(1,128)}, u32[]{:S(2)}) copy-start(f32[1,48]{1,0:T(1,128)} %param.19) | copy-start | bytes 580
  7.2 9.1 %copy-start.14 = (f32[1,48]{1,0:T(1,128)S(1)}, f32[1,48]{1,0:T(1,128)}, u32[]{:S(2)}) copy-start(f32[1,48]{1,0:T(1,128)} %param.18) | copy-start | bytes 580
  7.2 112.9 %all-gather.3.cloned.1.call-start = ((), (), s32[]{:S(2)}) async-start(), calls=%async_computation | async-start | bytes 21307392 | tf_op jit(solution)/shard_map/all_gather | solution.py:715
  12.7 191.1 %all-gather.5.cloned.1.call-start = ((), (), s32[]{:S(2)}) async-start(), calls=%async_computation.1 | async-start | bytes 10027008 | tf_op jit(solution)/shard_map/all_gather | solution.py:716
  239.4 20.9 %collective-permute-start = (bf16[256,1536]{1,0:T(8,128)(2,1)}, bf16[256,1536]{1,0:T(8,128)(2,1)S(1)}, u32[]{:S(2)}, u32[]{:S(2)}) collective-permute-start(bf16[256,1536]{1,0:T(8,128)(2,1)} %get-tuple-element.55), channel_id=1, source_target_pairs={{0,16},{1,17},{2,18},{3,19},{4,20},{5,21},{6,22},{7,23},{8,24},{9,... | collective-permute-start | bytes 2359304 | tf_op jit(solution)/shard_map/ppermute | solution.py:694
  260.3 0.9 copy-start.4
  295.8 21.0 %collective-permute-start.1 = (bf16[256,1536]{1,0:T(8,128)(2,1)}, bf16[256,1536]{1,0:T(8,128)(2,1)S(1)}, u32[]{:S(2)}, u32[]{:S(2)}) collective-permute-start(bf16[256,1536]{1,0:T(8,128)(2,1)} %get-tuple-element.63), channel_id=1, source_target_pairs={{0,16},{1,17},{2,18},{3,19},{4,20},{5,21},{6,22},{7,23},{8,24},{9,... | collective-permute-start | bytes 2359304 | tf_op jit(solution)/shard_map/ppermute | solution.py:694
  316.8 0.9 copy-start.3
  352.3 48.2 %copy-start = (bf16[3,256,1536]{2,1,0:T(8,128)(2,1)S(1)}, bf16[3,256,1536]{2,1,0:T(8,128)(2,1)}, u32[]{:S(2)}) copy-start(bf16[3,256,1536]{2,1,0:T(8,128)(2,1)} %get-tuple-element.85) | copy-start | bytes 7077892
  393.4 20.2 %collective-permute-start.2 = (bf16[256,1536]{1,0:T(8,128)(2,1)}, bf16[256,1536]{1,0:T(8,128)(2,1)S(1)}, u32[]{:S(2)}, u32[]{:S(2)}) collective-permute-start(bf16[256,1536]{1,0:T(8,128)(2,1)} %get-tuple-element.76), channel_id=1, source_target_pairs={{16,0},{17,1},{18,2},{19,3},{20,4},{21,5},{22,6},{23,7},{24,8},{25... | collective-permute-start | bytes 2359304 | tf_op jit(solution)/shard_map/ppermute | solution.py:694
  400.5 4.0 copy-start.10
  400.5 4.0 copy-start.11
  400.5 4.0 copy-start.12
  413.6 0.9 copy-start.5
  455.1 19.3 %collective-permute-start.3 = (bf16[256,1536]{1,0:T(8,128)(2,1)}, bf16[256,1536]{1,0:T(8,128)(2,1)S(1)}, u32[]{:S(2)}, u32[]{:S(2)}) collective-permute-start(bf16[256,1536]{1,0:T(8,128)(2,1)} %get-tuple-element.80), channel_id=1, source_target_pairs={{16,0},{17,1},{18,2},{19,3},{20,4},{21,5},{22,6},{23,7},{24,8},{25... | collective-permute-start | bytes 2359304 | tf_op jit(solution)/shard_map/ppermute | solution.py:694
  474.3 0.9 copy-start.6
  475.2 40.9 %copy-start.7 = (f32[8,3328]{1,0:T(8,128)S(1)}, f32[8,3328]{1,0:T(8,128)}, u32[]{:S(2)}) copy-start(f32[8,3328]{1,0:T(8,128)} %get-tuple-element.89) | copy-start | bytes 319492
  475.2 40.9 %copy-start.8 = (f32[8,3328]{1,0:T(8,128)S(1)}, f32[8,3328]{1,0:T(8,128)}, u32[]{:S(2)}) copy-start(f32[8,3328]{1,0:T(8,128)} %get-tuple-element.90) | copy-start | bytes 319492
  689.3 6.5 copy-start.1
  695.8 1.7 copy-start.2
Sparse Core Ops, SparseCore 0:
  12.9 107.2 all-gather.2
  122.4 81.4 all-gather.4

commit v3 on v2

v3 whole, which is shorter than its diff:
```python
import functools

import jax
import jax.numpy as jnp
from jax import lax
from jax.experimental import pallas as pl
from jax.experimental.pallas import tpu as pltpu
from jax.sharding import PartitionSpec as P

EPS = 1e-05
F32 = jnp.float32
BF16 = jnp.bfloat16
LANE = 128
LOG2E = 1.4426950408889634
NEG = -1e30
VMEM_LIMIT = 60 * 1024 * 1024
HIGH = lax.Precision.HIGHEST
MIXER_VMEM = 63 * 1024 * 1024
IN_TILE = 384
OUT_TILE = 256


def dot_nn(a, b, precision=None):
    return lax.dot_general(
        a, b, (((1,), (0,)), ((), ())), preferred_element_type=F32, precision=precision
    )


def dot_nt(a, b, precision=None):
    return lax.dot_general(
        a, b, (((1,), (1,)), ((), ())), preferred_element_type=F32, precision=precision
    )


def dot_tn(a, b, precision=None):
    return lax.dot_general(
        a, b, (((0,), (0,)), ((), ())), preferred_element_type=F32, precision=precision
    )


def sigmoid(v):
    return 1.0 / (1.0 + jnp.exp(-v))


def iota(shape, dim):
    return lax.broadcasted_iota(jnp.int32, shape, dim)


def row_sum(v):
    return jnp.sum(v, axis=1, keepdims=True)


def col_sum(v):
    return jnp.sum(v, axis=0, keepdims=True)


def segments_of(position, first_end, second_end):
    return (position >= first_end).astype(jnp.int32) + (position >= second_end).astype(jnp.int32)


def decay_terms(dt_raw, hp_ref, rows):
    z = dt_raw + hp_ref[0:1, :]
    step = jnp.maximum(z, 0.0) + jnp.log1p(jnp.exp(-jnp.abs(z)))
    below = (iota((rows, rows), 1) <= iota((rows, rows), 0)).astype(F32)
    ld = dot_nn(below, step * (hp_ref[1:2, :] * LOG2E), HIGH)
    lr = ld - jnp.log2(jnp.maximum(step, 1e-37))
    return z, step, ld, lr


def to_rows(v, out_ref, pairs):
    vt = v.T
    for p in range(pairs):
        out_ref[p, 0:2, :] = vt[2 * p : 2 * p + 2, :]


def pair_lanes(ref, p):
    return pltpu.roll(ref[...], lax.rem(LANE - 2 * p, LANE), 1)


def mixer_kernel(
    ends, x_hbm, cot_hbm, win_hbm, wout_hbm, par_ref, hp_ref,
    out_hbm, ing_hbm, nin_hbm, nout_hbm, gproj_hbm, gbr_hbm, proj_hbm, csum_hbm, mixed_hbm,
    pack_ref, stat_ref,
    win, wout, xs, cot, recv, sent, nin, nout, gbr, gproj, proj, csum, mixed, wide_s, stage,
    act_bc, cols_s, rows_s, row_q, col_q, cb, dcb, maskb, stat,
    load_sem, weight_sem, save_sem, store_sem, send_sem, recv_sem,
):
    section = lax.axis_index("section")
    me = lax.axis_index("dp")
    micros = x_hbm.shape[0]
    rows, d = nin.shape
    di, cw = mixed.shape[1], csum.shape[1]
    half = rows // 2
    pairs = di // LANE
    wide = proj.shape[1]
    lane = iota((rows, LANE), 1)
    first = lane < LANE // 2
    pos = iota((rows, LANE), 0)
    x_loads = [pltpu.make_async_copy(x_hbm.at[m], xs.at[m], load_sem.at[m]) for m in range(micros)]
    cot_loads = [
        pltpu.make_async_copy(cot_hbm.at[m], cot.at[m], load_sem.at[micros + m]) for m in range(micros)
    ]

    def tile(j, size):
        return pl.ds(pl.multiple_of(j * size, size), size)

    def weight_load(c):
        return pltpu.make_async_copy(
            win_hbm.at[:, tile(c, IN_TILE)], win.at[:, tile(c, IN_TILE)], weight_sem.at[c]
        )

    out_load = pltpu.make_async_copy(wout_hbm, wout, weight_sem.at[wide // IN_TILE])
    saves = [
        pltpu.make_async_copy(v, to, save_sem.at[i])
        for i, (v, to) in enumerate(((proj, proj_hbm), (csum, csum_hbm), (mixed, mixed_hbm)))
    ]
    restores = [
        pltpu.make_async_copy(to, v, save_sem.at[i])
        for i, (v, to) in enumerate(((proj, proj_hbm), (csum, csum_hbm), (mixed, mixed_hbm)))
    ]

    results = (
        (nin, nin_hbm), (nout, nout_hbm), (stage, out_hbm),
        (gbr, gbr_hbm), (gproj, gproj_hbm), (stage, ing_hbm),
    )

    def store(m, i):
        return pltpu.make_async_copy(results[i][0], results[i][1].at[m], store_sem.at[i])

    def hand_over(m, j):
        part = tile(j, OUT_TILE)
        return pltpu.make_async_remote_copy(
            src_ref=sent.at[m, :, part],
            dst_ref=recv.at[m, :, part],
            send_sem=send_sem.at[m, j],
            recv_sem=recv_sem.at[m, j],
            device_id=(1 - section, me),
            device_id_type=pl.DeviceIdType.MESH,
        )

    hands = d // OUT_TILE

    def repeat(count, body):
        def step(i, carry):
            body(i)
            return carry

        lax.fori_loop(0, count, step, 0)

    for copy in x_loads + cot_loads:
        copy.start()
    repeat(wide // IN_TILE, lambda c: weight_load(c).start())
    out_load.start()
    recv[...] = jnp.zeros_like(recv)
    pack_ref[...] = jnp.zeros_like(pack_ref)
    stat_ref[...] = jnp.zeros_like(stat_ref)
    barrier = pltpu.get_barrier_semaphore()
    pl.semaphore_signal(barrier, inc=1, device_id=(1 - section, me), device_id_type=pl.DeviceIdType.MESH)
    pl.semaphore_wait(barrier, 1)

    def input_of(m, cols):
        u = xs[m, :, cols].astype(F32)
        return u + jnp.where(section == 1, recv[m, :, cols].astype(F32), 0.0)

    def set_mask(e1, e2, upper):
        rpos, cpos = iota((rows, rows), 0), iota((rows, rows), 1)
        keep = (rpos <= cpos) if upper else (rpos >= cpos)
        keep &= segments_of(rpos, e1, e2) == segments_of(cpos, e1, e2)
        maskb[...] = jnp.where(keep, 0.0, NEG)

    def forward(m):
        e1, e2 = ends[m, 0], ends[m, 1]
        x_loads[m].wait()

        @pl.when(section == 1)
        def _():
            repeat(hands, lambda j: hand_over(m, j).wait_recv())

        u = input_of(m, slice(None))
        q = lax.rsqrt(jnp.mean(u * u, axis=1, keepdims=True) + EPS)
        if m > 0:
            for copy in [store(m - 1, i) for i in range(3)] + saves:
                copy.wait()
        nin[...] = (u * q * par_ref[7:8, :d]).astype(BF16)
        store(m, 0).start()

        def project(c):
            if m == 0:
                weight_load(c).wait()
            proj[:, tile(c, IN_TILE)] = dot_nn(nin[...], win[:, tile(c, IN_TILE)])

        repeat(wide // IN_TILE, project)
        if m < micros - 1:
            saves[0].start()
        dist = pos - jnp.where(pos >= e2, e2, jnp.where(pos >= e1, e1, 0))

        def conv_tile(j):
            here = tile(j, LANE)
            v = proj[:, pl.ds(pl.multiple_of(di + j * LANE, LANE), LANE)]
            acc = par_ref[4:5, here] + par_ref[3:4, here] * v
            for lag in range(1, 4):
                acc += par_ref[3 - lag : 4 - lag, here] * jnp.where(
                    dist >= lag, pltpu.roll(v, lag, 0), 0.0
                )
            csum[:, here] = acc

        repeat(cw // LANE, conv_tile)
        if m < micros - 1:
            saves[1].start()
        _, _, ld, lr = decay_terms(proj[:, di + cw :], hp_ref, rows)
        cols_s[...] = ld
        to_rows(lr, rows_s, pairs)
        for j in range(2):
            v = csum[:, di + j * LANE : di + (j + 1) * LANE]
            act_bc[j] = v * sigmoid(v)
        cb[...] = dot_nt(act_bc[1], act_bc[0], HIGH)
        set_mask(e1, e2, False)

        def pair(p, sq):
            here = tile(p, LANE)
            cs = csum[:, here]
            x = cs * sigmoid(cs)
            ldr = pair_lanes(cols_s, p)
            y0 = jnp.zeros((half, LANE), F32)
            y1 = jnp.zeros((half, LANE), F32)
            for h in range(2):
                xm = jnp.where(first if h == 0 else ~first, x, 0.0).astype(BF16)
                lc = ldr[:, h : h + 1]
                lrow = rows_s[p, h : h + 1, :]
                m0 = jnp.exp2((lc[:half] - lrow[:, :half]) + maskb[:half, :half]) * cb[:half, :half]
                m1 = jnp.exp2((lc[half:] - lrow) + maskb[half:, :]) * cb[half:, :]
                y0 += dot_nn(m0.astype(BF16), xm[:half])
                y1 += dot_nn(m1.astype(BF16), xm)
            y = jnp.concatenate([y0, y1], axis=0) + par_ref[6:7, here] * x
            mixed[:, here] = y
            gate = proj[:, here]
            g = y * (gate * sigmoid(gate))
            wide_s[:, here] = g
            return sq + g * g

        sq = lax.fori_loop(0, pairs, pair, jnp.zeros((rows, LANE), F32))
        if m < micros - 1:
            saves[2].start()
        r = lax.rsqrt(row_sum(sq) * (1.0 / di) + EPS)
        nout[...] = (wide_s[...] * r * par_ref[5:6, :di]).astype(BF16)
        store(m, 1).start()
        if m == 0:
            out_load.wait()
        valid = iota((rows, 1), 0) < e2

        def branch_tile(j):
            here = tile(j, OUT_TILE)
            branch = dot_nt(nout[...], wout[here, :])
            u = input_of(m, here)
            stage[:, here] = u + branch

            @pl.when(section == 0)
            def _():
                sent[m, :, here] = branch.astype(BF16)
                hand_over(m, j).start()

            usq = col_sum(row_sum(jnp.where(valid, u * u, 0.0)))
            bsq = col_sum(row_sum(jnp.where(valid, branch * branch, 0.0)))
            at = iota((8, LANE), 1)
            stat_ref[...] += jnp.where(at == 0, usq, jnp.where(at == 1, bsq, 0.0))

        repeat(hands, branch_tile)
        store(m, 2).start()

    def backward(m):
        e1, e2 = ends[m, 0], ends[m, 1]
        newest = m == micros - 1

        @pl.when(section == 0)
        def _():
            repeat(hands, lambda j: hand_over(m, j).wait_recv())

        cot_loads[m].wait()
        valid = (iota((rows, 1), 0) < e2).astype(F32)
        if not newest:
            store(m + 1, 3).wait()
        gbr[...] = jnp.where(
            section == 1, cot[m].astype(F32) * valid, recv[m].astype(F32)
        ).astype(BF16)
        store(m, 3).start()
        if not newest:
            for copy in restores:
                copy.wait()

        def gate_tile(c, carry):
            gn = dot_nn(gbr[...], wout[:, tile(c, IN_TILE)])
            wide_s[:, tile(c, IN_TILE)] = gn
            sq, cross = carry
            for j in range(IN_TILE // LANE):
                here = pl.ds(pl.multiple_of(c * IN_TILE + j * LANE, LANE), LANE)
                gate = proj[:, here]
                gated = mixed[:, here] * (gate * sigmoid(gate))
                sq += gated * gated
                cross += gated * (par_ref[5:6, here] * gn[:, j * LANE : (j + 1) * LANE])
            return sq, cross

        zero = jnp.zeros((rows, LANE), F32)
        sq, cross = lax.fori_loop(0, di // IN_TILE, gate_tile, (zero, zero))
        r = lax.rsqrt(row_sum(sq) * (1.0 / di) + EPS)
        rc = r * r * r * (row_sum(cross) * (1.0 / di))
        stat[0] = jnp.broadcast_to(r, (rows, LANE))
        stat[1] = jnp.broadcast_to(rc, (rows, LANE))
        z, dt, ld, lr = decay_terms(proj[:, di + cw :], hp_ref, rows)
        cols_s[...] = lr
        to_rows(ld, rows_s, pairs)
        for j in range(2):
            v = csum[:, di + j * LANE : di + (j + 1) * LANE]
            act_bc[j] = v * sigmoid(v)
        cb[...] = dot_nt(act_bc[0], act_bc[1], HIGH)
        set_mask(e1, e2, True)
        dcb[...] = jnp.zeros_like(dcb)
        col_q[...] = jnp.zeros_like(col_q)
        ahead = jnp.where(pos < e1, e1, jnp.where(pos < e2, e2, rows)) - pos
        if not newest:
            store(m + 1, 4).wait()

        def conv_back(dcv, off):
            here = pl.ds(off, LANE)
            there = pl.ds(pl.multiple_of(di + off, LANE), LANE)
            v = proj[:, there]
            out = par_ref[3:4, here] * dcv
            pack_ref[3:4, here] += col_sum(dcv * v)
            pack_ref[4:5, here] += col_sum(dcv)
            for lag in range(1, 4):
                moved = jnp.where(ahead > lag, pltpu.roll(dcv, rows - lag, 0), 0.0)
                out += par_ref[3 - lag : 4 - lag, here] * moved
                pack_ref[3 - lag : 4 - lag, here] += col_sum(moved * v)
            gproj[:, there] = out.astype(BF16)

        def pair(p):
            off = pl.multiple_of(p * LANE, LANE)
            here = pl.ds(off, LANE)
            gate = proj[:, here]
            mx = mixed[:, here]
            gnt = wide_s[:, here]
            sg = sigmoid(gate)
            sil = gate * sg
            gated = mx * sil
            pack_ref[5:6, here] += col_sum(gated * stat[0] * gnt)
            gg = stat[0] * (par_ref[5:6, here] * gnt) - gated * stat[1]
            dy = gg * sil
            gproj[:, here] = (gg * mx * (sg * (1.0 + gate * (1.0 - sg)))).astype(BF16)
            cs = csum[:, here]
            sc = sigmoid(cs)
            x = cs * sc
            pack_ref[6:7, here] += col_sum(dy * x)
            xb = x.astype(BF16)
            lrr = pair_lanes(cols_s, p)
            dx0 = jnp.zeros((half, LANE), F32)
            dx1 = jnp.zeros((half, LANE), F32)
            for h in range(2):
                dym = jnp.where(first if h == 0 else ~first, dy, 0.0).astype(BF16)
                lc = lrr[:, h : h + 1]
                lrow = rows_s[p, h : h + 1, :]
                d0 = jnp.exp2((lrow - lc[:half]) + maskb[:half, :])
                d1 = jnp.exp2((lrow[:, half:] - lc[half:]) + maskb[half:, half:])
                t0 = dot_nt(xb[:half], dym) * d0
                t1 = dot_nt(xb[half:], dym[half:]) * d1
                dx0 += dot_nn((d0 * cb[:half, :]).astype(BF16), dym)
                dx1 += dot_nn((d1 * cb[half:, half:]).astype(BF16), dym[half:])
                dcb[:half, :] += t0
                dcb[half:, half:] += t1
                q0 = t0 * cb[:half, :]
                q1 = t1 * cb[half:, half:]
                row_q[p, h : h + 1, :half] = col_sum(q0[:, :half])
                row_q[p, h : h + 1, half:] = col_sum(q0[:, half:]) + col_sum(q1)
                picked = lane == 2 * p + h
                col_q[:half, :] = jnp.where(picked[:half], row_sum(q0), col_q[:half, :])
                col_q[half:, :] = jnp.where(picked[half:], row_sum(q1), col_q[half:, :])
            dx = jnp.concatenate([dx0, dx1], axis=0) + par_ref[6:7, here] * dy
            conv_back(dx * (sc * (1.0 + cs * (1.0 - sc))), off)

        repeat(pairs, pair)
        total = dcb[...]
        for j, grad in enumerate((dot_nn(total, act_bc[1], HIGH), dot_tn(total, act_bc[0], HIGH))):
            cs = csum[:, di + j * LANE : di + (j + 1) * LANE]
            sc = sigmoid(cs)
            conv_back(grad * (sc * (1.0 + cs * (1.0 - sc))), di + j * LANE)
        spread = jnp.concatenate(
            [row_q[p, 0:2, :] for p in range(pairs)]
            + [jnp.zeros((LANE - 2 * pairs, rows), F32)],
            axis=0,
        )
        colq = col_q[...]
        above = (iota((rows, rows), 1) >= iota((rows, rows), 0)).astype(F32)
        after = dot_nn(above, spread.T - colq, HIGH)
        sz = sigmoid(z)
        ratio = jnp.where(z < -20.0, 1.0, sz / jnp.maximum(dt, 1e-37))
        neg_rate = hp_ref[1:2, :]
        ddt = jnp.where(lane < 2 * pairs, colq * ratio + neg_rate * after * sz, 0.0)
        gproj[:, di + cw :] = ddt.astype(BF16)
        pack_ref[7:8, d : d + LANE] += col_sum(ddt)
        pack_ref[7:8, d + LANE : d + 2 * LANE] += col_sum(
            jnp.where(lane < 2 * pairs, neg_rate * dt * after, 0.0)
        )
        store(m, 4).start()
        if m > 0:
            for copy in restores:
                copy.start()
        if newest:
            store(m, 2).wait()
        else:
            store(m + 1, 5).wait()

        def back_tile(j):
            stage[:, tile(j, OUT_TILE)] = dot_nt(gproj[...], win[tile(j, OUT_TILE), :])

        repeat(hands, back_tile)
        u = input_of(m, slice(None))
        q = lax.rsqrt(jnp.mean(u * u, axis=1, keepdims=True) + EPS)
        gi = stage[...]
        uq3 = q * q * q * jnp.mean(u * (par_ref[7:8, :d] * gi), axis=1, keepdims=True)
        pack_ref[7:8, :d] += col_sum(u * q * gi)

        def end_tile(j):
            here = tile(j, OUT_TILE)
            grad = (
                gbr[:, here].astype(F32)
                + q * (par_ref[7:8, here] * stage[:, here])
                - input_of(m, here) * uq3
            )
            stage[:, here] = grad

            @pl.when(section == 1)
            def _():
                sent[m, :, here] = grad.astype(BF16)
                hand_over(m, j).start()

        repeat(hands, end_tile)
        store(m, 5).start()

    for m in range(micros):
        forward(m)
    for i in range(2):
        store(micros - 1, i).wait()
    for m in reversed(range(micros)):
        backward(m)
    for i in range(3, 6):
        store(0, i).wait()
    for m in range(micros):
        repeat(hands, lambda j: hand_over(m, j).wait_send())


def mixer_steps(ends, x_in, cot, w_in, w_out_t, par, hp):
    micros, rows, d = x_in.shape
    di = w_out_t.shape[1]
    wide = w_in.shape[1]
    cw = par.shape[1]
    pairs = di // LANE
    hands = d // OUT_TILE
    hbm = pl.BlockSpec(memory_space=pl.ANY)
    vmem = pl.BlockSpec(memory_space=pltpu.VMEM)

    def stack(width, dtype):
        return jax.ShapeDtypeStruct((micros, rows, width), dtype)

    return pl.pallas_call(
        mixer_kernel,
        in_specs=[pl.BlockSpec(memory_space=pltpu.SMEM)] + [hbm] * 4 + [vmem] * 2,
        out_specs=[hbm] * 9 + [vmem] * 2,
        out_shape=[
            stack(d, F32), stack(d, F32), stack(d, BF16), stack(di, BF16), stack(wide, BF16), stack(d, BF16),
            jax.ShapeDtypeStruct((rows, wide), F32),
            jax.ShapeDtypeStruct((rows, cw), F32),
            jax.ShapeDtypeStruct((rows, di), F32),
            jax.ShapeDtypeStruct((8, cw), F32),
            jax.ShapeDtypeStruct((8, LANE), F32),
        ],
        scratch_shapes=[
            pltpu.VMEM((d, wide), BF16),
            pltpu.VMEM((d, di), BF16),
            pltpu.VMEM((micros, rows, d), BF16),
            pltpu.VMEM((micros, rows, d), BF16),
            pltpu.VMEM((micros, rows, d), BF16),
            pltpu.VMEM((micros, rows, d), BF16),
            pltpu.VMEM((rows, d), BF16),
            pltpu.VMEM((rows, di), BF16),
            pltpu.VMEM((rows, d), BF16),
            pltpu.VMEM((rows, wide), BF16),
            pltpu.VMEM((rows, wide), F32),
            pltpu.VMEM((rows, cw), F32),
            pltpu.VMEM((rows, di), F32),
            pltpu.VMEM((rows, di), F32),
            pltpu.VMEM((rows, d), F32),
            pltpu.VMEM((2, rows, LANE), F32),
            pltpu.VMEM((rows, LANE), F32),
            pltpu.VMEM((pairs, 8, rows), F32),
            pltpu.VMEM((pairs, 8, rows), F32),
            pltpu.VMEM((rows, LANE), F32),
            pltpu.VMEM((rows, rows), F32),
            pltpu.VMEM((rows, rows), F32),
            pltpu.VMEM((rows, rows), F32),
            pltpu.VMEM((2, rows, LANE), F32),
            pltpu.SemaphoreType.DMA((2 * micros,)),
            pltpu.SemaphoreType.DMA((wide // IN_TILE + 1,)),
            pltpu.SemaphoreType.DMA((3,)),
            pltpu.SemaphoreType.DMA((6,)),
            pltpu.SemaphoreType.DMA((micros, hands)),
            pltpu.SemaphoreType.DMA((micros, hands)),
        ],
        compiler_params=pltpu.CompilerParams(
            collective_id=1, has_side_effects=True, vmem_limit_bytes=MIXER_VMEM
        ),
        cost_estimate=pl.CostEstimate(
            flops=12 * rows * d * (wide + di), bytes_accessed=100 << 20, transcendentals=16 << 20
        ),
        name="mixer_steps",
    )(ends, x_in, cot, w_in, w_out_t, par, hp)


def ring_place(index, n):
    chip, core = index // 2, index % 2
    z, x = chip // 2, chip % 2
    return 2 * ((1 - x) * z + x * (n // 2 - 1 - z)) + core


def ring_device(place, n):
    spot, core = place // 2, place % 2
    far = spot // (n // 4)
    chip = (1 - far) * (2 * spot) + far * (2 * (n // 2 - 1 - spot) + 1)
    return 2 * chip + core


def tile_chunks(columns, parts):
    tiles = columns // LANE
    cuts = [LANE * (-(-tiles * i // parts)) for i in range(parts + 1)]
    return [(cuts[i], cuts[i + 1] - cuts[i]) for i in range(parts)]


def greet_all(n, me, section):
    barrier = pltpu.get_barrier_semaphore()

    def signal(i, carry):
        pl.semaphore_signal(
            barrier, inc=1, device_id=(section, (me + i) % n), device_id_type=pl.DeviceIdType.MESH
        )
        return carry

    lax.fori_loop(1, n, signal, 0)
    pl.semaphore_wait(barrier, n - 1)


def scatter_kernel(
    n, nin_t, gbr_t, gproj_hbm, nout_hbm, small_ref,
    gin_ref, gout_ref, small_out,
    gproj, nout, held, small_got, load_sem, send_sem, recv_sem, small_send, small_recv,
):
    me = lax.axis_index("dp")
    section = lax.axis_index("section")
    place = ring_place(me, n)
    steps = n // 2
    micros, rows = gproj_hbm.shape[0], gproj_hbm.shape[1]
    wide, di = gproj.shape[1], nout.shape[1]
    targets = (ring_device((place + 1) % n, n), ring_device((place + n - 1) % n, n))
    loads = []
    for m in range(micros):
        part = pl.ds(m * rows, rows)
        loads.append(pltpu.make_async_copy(nout_hbm.at[m], nout.at[part], load_sem.at[0, m]))
        loads.append(pltpu.make_async_copy(gproj_hbm.at[m], gproj.at[part], load_sem.at[1, m]))
    for load in loads:
        load.start()
    greet_all(n, me, section)

    def small_copy(other, slot):
        return pltpu.make_async_remote_copy(
            src_ref=small_ref.at[other],
            dst_ref=small_got.at[slot],
            send_sem=small_send.at[slot],
            recv_sem=small_recv.at[slot],
            device_id=(section, other),
            device_id_type=pl.DeviceIdType.MESH,
        )

    def small_start(i, carry):
        small_copy((me + i) % n, i).start()
        return carry

    lax.fori_loop(1, n, small_start, 0)
    for load in loads:
        load.wait()

    out_cuts = tile_chunks(di, 2)
    in_cuts = tile_chunks(wide, 4)
    chunks = [
        (False, *out_cuts[0]), (False, *out_cuts[1]),
        (True, *in_cuts[0]), (True, *in_cuts[2]), (True, *in_cuts[1]), (True, *in_cuts[3]),
    ]

    def own(owner, chunk):
        is_in, start, size = chunk
        if is_in:
            return dot_nn(nin_t[owner], gproj[:, start : start + size])
        return dot_nn(gbr_t[owner], nout[:, start : start + size])

    def columns(chunk):
        is_in, start, size = chunk
        return pl.ds(start if is_in else wide + start, size)

    def owner_of(way, k):
        shift = steps - k if way == 0 else n - steps + k
        return ring_device((place + shift) % n, n)

    def send(way, k, c):
        cols = columns(chunks[c])
        return pltpu.make_async_remote_copy(
            src_ref=held.at[way, k, :, cols],
            dst_ref=held.at[way, k + 1, :, cols],
            send_sem=send_sem.at[way, k, c],
            recv_sem=recv_sem.at[way, k, c],
            device_id=(section, targets[way]),
            device_id_type=pl.DeviceIdType.MESH,
        )

    def run_step(k, first, second):
        for c, chunk in enumerate(chunks):
            for way in range(2):
                if first and c % 2 != way:
                    continue
                cols = columns(chunk)
                total = own(owner_of(way, k), chunk)
                if not first and not (second and c % 2 != way):
                    send(way, k - 1, c).wait_recv()
                    total += held[way, k, :, cols].astype(F32)
                held[way, k, :, cols] = total.astype(BF16)
                send(way, k, c).start()

    run_step(0, True, False)
    run_step(1, False, True)

    def loop(k, carry):
        run_step(k, False, False)
        return carry

    lax.fori_loop(2, steps, loop, 0)

    for c, chunk in enumerate(chunks):
        is_in, start, size = chunk
        cols = columns(chunk)
        total = own(me, chunk)
        for way in range(2):
            send(way, steps - 1, c).wait_recv()
            total += held[way, steps, :, cols].astype(F32)
        if is_in:
            gin_ref[:, start : start + size] = total
        else:
            gout_ref[:, start : start + size] = total

    small_out[...] = small_ref[me]

    def small_end(i, carry):
        copy = small_copy((me + i) % n, i)
        copy.wait()
        small_out[...] += small_got[i]
        return carry

    lax.fori_loop(1, n, small_end, 0)
    for c in range(len(chunks)):
        send(c % 2, 0, c).wait_send()

    def sent(k, carry):
        for c in range(len(chunks)):
            for way in range(2):
                send(way, k, c).wait_send()
        return carry

    lax.fori_loop(1, steps, sent, 0)


def scatter_gradients(n, nin_t, gbr_t, gproj, nout, small):
    piece, tokens = nin_t.shape[1:]
    wide, di = gproj.shape[2], nout.shape[2]
    micros = nout.shape[0]
    steps = n // 2
    vmem = pl.BlockSpec(memory_space=pltpu.VMEM)
    hbm = pl.BlockSpec(memory_space=pl.ANY)
    return pl.pallas_call(
        functools.partial(scatter_kernel, n),
        out_shape=[
            jax.ShapeDtypeStruct((piece, wide), F32),
            jax.ShapeDtypeStruct((piece, di), F32),
            jax.ShapeDtypeStruct(small.shape[1:], F32),
        ],
        in_specs=[vmem, vmem, hbm, hbm, vmem],
        out_specs=[vmem, vmem, vmem],
        scratch_shapes=[
            pltpu.VMEM((tokens, wide), BF16),
            pltpu.VMEM((tokens, di), BF16),
            pltpu.VMEM((2, steps + 1, piece, wide + di), BF16),
            pltpu.VMEM(small.shape, F32),
            pltpu.SemaphoreType.DMA((2, micros)),
            pltpu.SemaphoreType.DMA((2, steps, 6)),
            pltpu.SemaphoreType.DMA((2, steps, 6)),
            pltpu.SemaphoreType.DMA((n,)),
            pltpu.SemaphoreType.DMA((n,)),
        ],
        compiler_params=pltpu.CompilerParams(
            collective_id=0, has_side_effects=True, vmem_limit_bytes=VMEM_LIMIT
        ),
        cost_estimate=pl.CostEstimate(
            flops=2 * n * piece * tokens * (wide + di), bytes_accessed=20 << 20, transcendentals=0
        ),
        name="gradient_scatter",
    )(nin_t, gbr_t, gproj, nout, small)


def shards(
    x_in, lengths, norm_pre, w_in, conv_w, conv_b, dt_bias, a_log, skip_scale, norm_gate, w_out, cotangent
):
    micros, rows, d = x_in.shape
    heads = dt_bias.shape[1]
    taps = conv_w.shape[1]
    devices = lax.axis_size("dp")
    piece, wide = w_in.shape[1], w_in.shape[2]
    di = w_out.shape[1]
    cw_piece, gate_piece = conv_w.shape[2], norm_gate.shape[1]
    cw = cw_piece * devices
    pad = LANE - heads

    small = jnp.concatenate(
        [norm_pre[0], conv_b[0], norm_gate[0], conv_w[0].reshape(-1)]
    )
    small = jnp.pad(small, (0, piece * pad - small.shape[0])).reshape(piece, pad)
    gathered_in = lax.all_gather(jnp.concatenate([w_in[0], small], axis=1), "dp", axis=0, tiled=True)
    gathered_out = lax.all_gather(w_out[0].T, "dp", axis=0, tiled=True)
    tails = gathered_in[:, wide:].reshape(devices, piece * pad).astype(F32)
    ends = [0]
    for size in (piece, cw_piece, gate_piece, taps * cw_piece):
        ends.append(ends[-1] + size)
    gain_pre = tails[:, ends[0] : ends[1]].reshape(-1)
    conv_bias = tails[:, ends[1] : ends[2]].reshape(-1)
    gate_gain = tails[:, ends[2] : ends[3]].reshape(-1)
    conv_taps = tails[:, ends[3] : ends[4]].reshape(devices, taps, cw_piece)
    conv_taps = conv_taps.transpose(1, 0, 2).reshape(taps, cw)

    def wide_row(v):
        return jnp.pad(v, (0, cw - v.shape[0]))[None]

    par = jnp.concatenate(
        [
            conv_taps,
            conv_bias[None],
            wide_row(gate_gain),
            wide_row(jnp.repeat(skip_scale[0], di // heads)),
            wide_row(gain_pre),
        ],
        axis=0,
    )
    hp = jnp.pad(jnp.stack([dt_bias[0], -jnp.exp(a_log[0])]), ((0, 6), (0, pad)))

    first_end = lengths[:, 0, 0]
    second_end = first_end + lengths[:, 0, 1]
    ends = jnp.stack([first_end, second_end], axis=1)
    (outputs, in_grad, normed_in, normed_out, grad_proj, grad_branch, _, _, _, packs, stats) = mixer_steps(
        ends, x_in, cotangent, gathered_in, gathered_out, par, hp
    )
    valid_total = jnp.sum(second_end).astype(F32)

    def turned(v):
        return v.reshape(micros * rows, d).T.reshape(devices, piece, micros * rows)

    me = lax.axis_index("dp")
    per_head = packs[6, :di].reshape(heads, di // heads).sum(axis=1)
    common = jnp.concatenate(
        [
            packs[7, d : d + heads],
            packs[7, d + LANE : d + LANE + heads],
            per_head,
            stats[0, :2],
            valid_total[None],
        ]
    )
    small = jnp.concatenate(
        [
            packs[:taps].reshape(taps, devices, cw_piece).transpose(1, 0, 2).reshape(devices, -1),
            packs[4].reshape(devices, cw_piece),
            packs[5, :di].reshape(devices, gate_piece),
            packs[7, :d].reshape(devices, piece),
            jnp.broadcast_to(common, (devices, common.shape[0])),
        ],
        axis=1,
    )
    small_rows = -(-small.shape[1] // (8 * LANE)) * 8
    small = jnp.pad(small, ((0, 0), (0, small_rows * LANE - small.shape[1])))
    in_shard, out_shard, small = scatter_gradients(
        devices, turned(normed_in), turned(grad_branch), grad_proj, normed_out,
        small.reshape(devices, small_rows, LANE),
    )
    small = small.reshape(-1)
    parts = []
    start = 0
    for size in (taps * cw_piece, cw_piece, gate_piece, piece, heads, heads, heads, 3):
        parts.append(small[start : start + size])
        start += size
    sums = parts[7]
    rms = jnp.sqrt(sums[:2] / (sums[2] * d))

    return (
        outputs[None],
        in_grad[None],
        parts[3][None],
        in_shard[None, :, :wide],
        parts[0].reshape(1, taps, cw_piece),
        parts[1][None],
        parts[4][None],
        parts[5][None],
        parts[6][None],
        parts[2][None],
        out_shard.T[None],
        rms[None],
    )


def solution(mesh):
    placed = (
        P(None, "dp", None),
        P(None, "dp", None),
        P("section", "dp"),
        P("section", "dp", None),
        P("section", None, "dp"),
        P("section", "dp"),
        P("section", None),
        P("section", None),
        P("section", None),
        P("section", "dp"),
        P("section", None, "dp"),
        P(None, "dp", None),
    )
    return jax.shard_map(
        shards,
        mesh=mesh,
        in_specs=placed,
        out_specs=(
            P("section", None, "dp", None),
            P("section", None, "dp", None),
            P("section", "dp"),
            P("section", "dp", None),
            P("section", None, "dp"),
            P("section", "dp"),
            P("section", None),
            P("section", None),
            P("section", None),
            P("section", "dp"),
            P("section", None, "dp"),
            P("section", None),
        ),
        check_vma=False,
    )
```

time: 715 us -> 607 us (0.85); the launches traced: 706 us -> 606 us
  waiting for transfers between devices: 236 us -> 185 us
  Pallas kernels: 387 us -> 365 us
  starting transfers between devices: 10.9 us -> 0.08 us
  local copies, waits for them, and re-layouts: 41.4 us -> 32 us
    ppermute x4 -> x0, waiting for transfers between devices: 51.4 us -> none  [passed_along(): return lax.ppermute(shard, axis, pairs)]
    pallas_call x6 -> x1, Pallas kernels: 226 us -> 205 us  [mixer_steps(): pl.pallas_call(mixer_kernel, in_specs=[pl.BlockSpec(memory_space=pltpu.SM...]
    ppermute x4 -> x0, starting transfers between devices: 10.8 us -> none  [passed_along(): return lax.ppermute(shard, axis, pairs)]
    broadcast_in_dim x2 -> x0, local copies, waits for them, and re-layouts: 7.66 us -> none  [the longest x1 3.91 us: shards(): in_grad[:micros][None]]
  transfers between devices with their start and end apart: 6 -> 2, of which waited for: 6 -> 2; matrix products, arithmetic and copies ran while one was open for 3% -> 1% of each run, Pallas kernels for 0% -> 0%
where the time goes in v3:
time: 607 us; the launch traced here: 606 us
  Pallas kernels  365 us (60%)
  waiting for transfers between devices  185 us (30%)
  local copies, waits for them, and re-layouts  32 us (5%)
  between operations  15.6 us (3%)
  other arithmetic  8.32 us (1%)
    pallas_call x1, Pallas kernels, mixer_steps(): pl.pallas_call(mixer_kernel, in_specs=[pl.BlockSpec(memory_space=pltpu.SM...  205 us
    pallas_call x1, Pallas kernels, scatter_gradients(): pl.pallas_call(functools.partial(scatter_kernel, n), out_shape=[jax.Shape...  160 us
    all_gather x1, waiting for transfers between devices, shards(): lax.all_gather(jnp.concatenate([w_in[0], small], axis=1), 'dp', axis=0, t...  104 us
    all_gather x1, waiting for transfers between devices, shards(): gathered_out = lax.all_gather(w_out[0].T, 'dp', axis=0, tiled=True)  80.6 us
  transfers between devices with their start and end apart: 2, of which 2 were waited for; matrix products, arithmetic and copies ran while one was open for 1% of the time, Pallas kernels for 0%

profile of v3, /device:TPU:0, one launch (start us, length us, event | category | flops | bytes accessed | tf_op | source)
XLA Modules:
  0.0 606.4 jit_solution(11923796163885044099)
XLA Ops:
  7.3 0.7 reduce.1
  8.0 0.7 reduce.2
  8.7 0.8 reshape_squeeze.15
  9.4 0.8 concatenate.15
  10.3 2.4 pad_maximum_fusion
  12.8 0.7 all-gather.5.cloned.1.call-update
  13.5 0.7 add_reduce_fusion
  16.3 103.8 %all-gather.3.cloned.1.call-done.win_hbm = bf16[1536,6528]{1,0:T(8,128)(2,1)} async-done(((bf16[96,6528]{1,0:T(8,128)(2,1)}), bf16[1536,6528]{1,0:T(8,128)(2,1)}) %all-gather.3.cloned.1.call-update) | async-done | bytes 20054032 | tf_op jit(solution)/shard_map/all_gather | solution.py:728
  120.1 1.2 slice_convert_fusion
  122.5 0.7 concatenate.17.par_ref
  123.2 80.6 %all-gather.5.cloned.1.call-done.wout_hbm = bf16[1536,3072]{1,0:T(8,128)(2,1)} async-done(((bf16[96,3072]{1,0:T(8,128)(2,1)}), bf16[1536,3072]{1,0:T(8,128)(2,1)}) %all-gather.5.cloned.1.call-update) | async-done | bytes 9437200 | tf_op jit(solution)/shard_map/all_gather | solution.py:729
  203.9 205.1 %mixer_steps.1 = (f32[2,256,1536]{2,1,0:T(8,128)}, f32[2,256,1536]{2,1,0:T(8,128)}, bf16[2,256,1536]{2,1,0:T(8,128)(2,1)}, bf16[2,256,3072]{2,1,0:T(8,128)(2,1)}...) custom-call(s32[2,2]{1,0:T(2,128)} %pad_add_fusion.ends, ...), custom_call_target="tpu_custom_call" | custom-call | flops 45298483200 | bytes 104857600 | tf_op jit(solution)/shard_map/mixer_steps/pallas_call | solution.py:462
  408.9 0.8 slice_bitcast_fusion.6
  409.7 0.8 slice_reduce_fusion.3
  410.6 0.9 slice_reduce_fusion
  411.5 1.0 slice_reduce_fusion.1
  412.5 0.9 slice.85
  415.7 2.6 copy.35
  418.3 1.6 copy.36
  419.9 160.3 %gradient_scatter.1 = (f32[96,6528]{1,0:T(8,128)}, f32[96,3072]{1,0:T(8,128)}, f32[16,128]{1,0:T(8,128)}) custom-call(bf16[16,96,512]{2,1,0:T(8,128)(2,1)} %bitcast.55, bf16[16,96,512]{2,1,0:T(8,128)(2,1)} %bitcast.56, bf16[2,256,6528]{2,1,0:T(8,128)(2,1)} %get-tuple-element.27.gproj_hbm, bf16[2,256,3072]{2,1,0:T(8,128)(2,1)} %get-tuple-element.28.nout_hbm, ...), custom_call_target="tpu_custom_call" | custom-call | flops 15099494400 | bytes 20971520 | tf_op jit(solution)/shard_map/gradient_scatter/pallas_call | solution.py:681
  580.2 1.3 slice.116
  581.4 1.3 slice_bitcast_fusion.4
  582.7 1.3 slice.114
  584.0 1.3 slice.110
  585.3 1.4 slice_bitcast_fusion.1
  586.7 0.7 slice.109
  588.0 1.3 fusion.1
  590.0 3.5 slice_bitcast_fusion
  593.5 1.7 copy.44
  595.1 1.4 copy-done
  596.5 1.7 copy.45
  598.6 1.0 copy.46
  (58 shorter events, 6.1 us)
Async XLA Ops:
  7.2 6.3 %copy-start.4 = (s32[2,1,2]{2,1,0:T(1,128)S(1)}, s32[2,1,2]{2,1,0:T(1,128)}, u32[]{:S(2)}) copy-start(s32[2,1,2]{2,1,0:T(1,128)} %param.13) | copy-start | bytes 52
  7.2 7.7 %copy-start.5 = (f32[1,48]{1,0:T(1,128)S(1)}, f32[1,48]{1,0:T(1,128)}, u32[]{:S(2)}) copy-start(f32[1,48]{1,0:T(1,128)} %param.20) | copy-start | bytes 580
  7.2 8.5 %copy-start.7 = (f32[1,48]{1,0:T(1,128)S(1)}, f32[1,48]{1,0:T(1,128)}, u32[]{:S(2)}) copy-start(f32[1,48]{1,0:T(1,128)} %param.19) | copy-start | bytes 580
  7.2 8.5 %copy-start.6 = (f32[1,48]{1,0:T(1,128)S(1)}, f32[1,48]{1,0:T(1,128)}, u32[]{:S(2)}) copy-start(f32[1,48]{1,0:T(1,128)} %param.18) | copy-start | bytes 580
  7.2 112.9 %all-gather.3.cloned.1.call-start = ((), (), s32[]{:S(2)}) async-start(), calls=%async_computation | async-start | bytes 21307392 | tf_op jit(solution)/shard_map/all_gather | solution.py:728
  12.7 191.1 %all-gather.5.cloned.1.call-start = ((), (), s32[]{:S(2)}) async-start(), calls=%async_computation.1 | async-start | bytes 10027008 | tf_op jit(solution)/shard_map/all_gather | solution.py:729
  408.9 9.4 %copy-start.2 = (bf16[2,256,1536]{2,1,0:T(8,128)(2,1)S(1)}, bf16[2,256,1536]{2,1,0:T(8,128)(2,1)}, u32[]{:S(2)}) copy-start(bf16[2,256,1536]{2,1,0:T(8,128)(2,1)} %get-tuple-element.26) | copy-start | bytes 4718596
  590.0 3.5 copy-start.1
  593.5 3.0 copy-start
  596.5 2.1 copy-start.3
Sparse Core Ops, SparseCore 0:
  12.9 107.2 all-gather.2
  122.4 81.4 all-gather.4

commit v4 on v3

--- a/solution.py
+++ b/solution.py
@@ -77,13 +77,32 @@
     return pltpu.roll(ref[...], lax.rem(LANE - 2 * p, LANE), 1)
 
 
+def ring_place(index, n):
+    chip, core = index // 2, index % 2
+    z, x = chip // 2, chip % 2
+    return 2 * ((1 - x) * z + x * (n // 2 - 1 - z)) + core
+
+
+def ring_device(place, n):
+    spot, core = place // 2, place % 2
+    far = spot // (n // 4)
+    chip = (1 - far) * (2 * spot) + far * (2 * (n // 2 - 1 - spot) + 1)
+    return 2 * chip + core
+
+
+def tile_chunks(columns, parts):
+    tiles = columns // LANE
+    cuts = [LANE * (-(-tiles * i // parts)) for i in range(parts + 1)]
+    return [(cuts[i], cuts[i + 1] - cuts[i]) for i in range(parts)]
+
+
 def mixer_kernel(
-    ends, x_hbm, cot_hbm, win_hbm, wout_hbm, par_ref, hp_ref,
+    n, ring, ends, x_hbm, cot_hbm, win_hbm, wout_hbm, par_in, small_ref, hp_ref,
     out_hbm, ing_hbm, nin_hbm, nout_hbm, gproj_hbm, gbr_hbm, proj_hbm, csum_hbm, mixed_hbm,
     pack_ref, stat_ref,
     win, wout, xs, cot, recv, sent, nin, nout, gbr, gproj, proj, csum, mixed, wide_s, stage,
-    act_bc, cols_s, rows_s, row_q, col_q, cb, dcb, maskb, stat,
-    load_sem, weight_sem, save_sem, store_sem, send_sem, recv_sem,
+    act_bc, cols_s, rows_s, row_q, col_q, cb, dcb, maskb, stat, par_ref, small_got,
+    load_sem, weight_sem, save_sem, store_sem, send_sem, recv_sem, hop_send, hop_recv, small_send, small_recv,
 ):
     section = lax.axis_index("section")
     me = lax.axis_index("dp")
@@ -104,12 +123,62 @@
     def tile(j, size):
         return pl.ds(pl.multiple_of(j * size, size), size)
 
-    def weight_load(c):
-        return pltpu.make_async_copy(
-            win_hbm.at[:, tile(c, IN_TILE)], win.at[:, tile(c, IN_TILE)], weight_sem.at[c]
+    place = ring_place(me, n) if ring else 0
+    steps = n // 2
+    piece = win_hbm.shape[0]
+    part = piece // 2
+    targets = (ring_device((place + 1) % n, n), ring_device((place + n - 1) % n, n)) if ring else None
+    shards_of = (win_hbm, wout_hbm)
+    wholes = (win, wout)
+
+    def own_load(which):
+        if ring:
+            to = wholes[which].at[tile(me, piece), :]
+        else:
+            to = wholes[which]
+        return pltpu.make_async_copy(shards_of[which], to, weight_sem.at[which])
+
+    def hop(which, way, k, c, sender):
+        shift = n - k if way == 0 else k
+        owner = ring_device((sender + shift) % n, n)
+        rows_of = pl.ds(pl.multiple_of(owner * piece + c * part, part), part)
+        return pltpu.make_async_remote_copy(
+            src_ref=wholes[which].at[rows_of, :],
+            dst_ref=wholes[which].at[rows_of, :],
+            send_sem=hop_send.at[which, way, k, c],
+            recv_sem=hop_recv.at[which, way, k, c],
+            device_id=(section, targets[way]),
+            device_id_type=pl.DeviceIdType.MESH,
         )
 
-    out_load = pltpu.make_async_copy(wout_hbm, wout, weight_sem.at[wide // IN_TILE])
+    def hop_arrived(which, way, k, c):
+        hop(which, way, k, c, place + n - 1 if way == 0 else place + 1).wait_recv()
+
+    def hops(which, k, start, take, last=False):
+        for c in range(2):
+            for way in range(2):
+                if take:
+                    hop_arrived(which, way, k - 1, c)
+                if start and not (last and c != way):
+                    hop(which, way, k, c, place).start()
+
+    def hop_middle(which, low, high):
+        repeat(high - low, lambda i: hops(which, low + i, True, True))
+
+    def hop_end(which):
+        for way in range(2):
+            hop_arrived(which, way, steps - 1, way)
+
+    def small_copy(source, target):
+        return pltpu.make_async_remote_copy(
+            src_ref=small_ref,
+            dst_ref=small_got.at[source],
+            send_sem=small_send.at[target],
+            recv_sem=small_recv.at[source],
+            device_id=(section, target),
+            device_id_type=pl.DeviceIdType.MESH,
+        )
+
     saves = [
         pltpu.make_async_copy(v, to, save_sem.at[i])
         for i, (v, to) in enumerate(((proj, proj_hbm), (csum, csum_hbm), (mixed, mixed_hbm)))
@@ -149,14 +218,68 @@
 
     for copy in x_loads + cot_loads:
         copy.start()
-    repeat(wide // IN_TILE, lambda c: weight_load(c).start())
-    out_load.start()
+    for which in range(2):
+        own_load(which).start()
     recv[...] = jnp.zeros_like(recv)
     pack_ref[...] = jnp.zeros_like(pack_ref)
     stat_ref[...] = jnp.zeros_like(stat_ref)
     barrier = pltpu.get_barrier_semaphore()
     pl.semaphore_signal(barrier, inc=1, device_id=(1 - section, me), device_id_type=pl.DeviceIdType.MESH)
-    pl.semaphore_wait(barrier, 1)
+    if ring:
+
+        def greet(i):
+            pl.semaphore_signal(
+                barrier,
+                inc=1,
+                device_id=(section, (me + i + 1) % n),
+                device_id_type=pl.DeviceIdType.MESH,
+            )
+
+        repeat(n - 1, greet)
+        pl.semaphore_wait(barrier, n)
+        own_load(0).wait()
+        hops(0, 0, True, False)
+        repeat(n - 1, lambda i: small_copy(me, (me + i + 1) % n).start())
+        hop_middle(0, 1, steps - 1)
+        hops(0, steps - 1, True, True, True)
+        own_load(1).wait()
+        hops(1, 0, True, False)
+        small_got[me] = small_ref[...]
+
+        def small_take(i):
+            other = (me + i + 1) % n
+            small_copy(other, other).wait_recv()
+
+        repeat(n - 1, small_take)
+        tap_cols, gate_cols, pre_cols = (v.shape[1] // n for v in (csum, mixed, nin))
+        joined = [small_got[o] for o in range(n)]
+        par_ref[...] = par_in[...]
+        par_ref[0:5, :] = jnp.concatenate([v[0:5, :tap_cols] for v in joined], axis=1)
+        par_ref[5:6, :di] = jnp.concatenate([v[5:6, :gate_cols] for v in joined], axis=1)
+        par_ref[7:8, :d] = jnp.concatenate([v[7:8, :pre_cols] for v in joined], axis=1)
+        hop_end(0)
+
+        @pl.when(section == 1)
+        def _():
+            hop_middle(1, 1, steps - 1)
+            hops(1, steps - 1, True, True, True)
+            hop_end(1)
+
+    else:
+        pl.semaphore_wait(barrier, 1)
+        par_ref[...] = par_in[...]
+        for which in range(2):
+            own_load(which).wait()
+
+    def early_hops(m, low, high):
+        if ring and m == 0:
+
+            @pl.when(section == 0)
+            def _():
+                hop_middle(1, low, min(high, steps - 1))
+                if high == steps:
+                    hops(1, steps - 1, True, True, True)
+                    hop_end(1)
 
     def input_of(m, cols):
         u = xs[m, :, cols].astype(F32)
@@ -185,8 +308,6 @@
         store(m, 0).start()
 
         def project(c):
-            if m == 0:
-                weight_load(c).wait()
             proj[:, tile(c, IN_TILE)] = dot_nn(nin[...], win[:, tile(c, IN_TILE)])
 
         repeat(wide // IN_TILE, project)
@@ -205,6 +326,7 @@
             csum[:, here] = acc
 
         repeat(cw // LANE, conv_tile)
+        early_hops(m, 1, 2)
         if m < micros - 1:
             saves[1].start()
         _, _, ld, lr = decay_terms(proj[:, di + cw :], hp_ref, rows)
@@ -238,14 +360,16 @@
             wide_s[:, here] = g
             return sq + g * g
 
-        sq = lax.fori_loop(0, pairs, pair, jnp.zeros((rows, LANE), F32))
+        sq = lax.fori_loop(0, pairs // 2, pair, jnp.zeros((rows, LANE), F32))
+        early_hops(m, 2, 3)
+        sq = lax.fori_loop(pairs // 2, pairs, pair, sq)
+        early_hops(m, 3, 4)
         if m < micros - 1:
             saves[2].start()
         r = lax.rsqrt(row_sum(sq) * (1.0 / di) + EPS)
         nout[...] = (wide_s[...] * r * par_ref[5:6, :di]).astype(BF16)
         store(m, 1).start()
-        if m == 0:
-            out_load.wait()
+        early_hops(m, 4, steps)
         valid = iota((rows, 1), 0) < e2
 
         def branch_tile(j):
@@ -444,14 +568,26 @@
         store(0, i).wait()
     for m in range(micros):
         repeat(hands, lambda j: hand_over(m, j).wait_send())
-
-
-def mixer_steps(ends, x_in, cot, w_in, w_out_t, par, hp):
+    if ring:
+        for which in range(2):
+            for way in range(2):
+                for c in range(2):
+                    count = steps if c == way else steps - 1
+                    repeat(count, lambda k: hop(which, way, k, c, place).wait_send())
+
+        def small_sent(i):
+            small_copy(me, (me + i + 1) % n).wait_send()
+
+        repeat(n - 1, small_sent)
+
+
+def mixer_steps(n, ring, ends, x_in, cot, w_in, w_out_t, par, small, hp):
     micros, rows, d = x_in.shape
     di = w_out_t.shape[1]
     wide = w_in.shape[1]
     cw = par.shape[1]
     pairs = di // LANE
+    steps = n // 2
     hands = d // OUT_TILE
     hbm = pl.BlockSpec(memory_space=pl.ANY)
     vmem = pl.BlockSpec(memory_space=pltpu.VMEM)
@@ -460,8 +596,8 @@
         return jax.ShapeDtypeStruct((micros, rows, width), dtype)
 
     return pl.pallas_call(
-        mixer_kernel,
-        in_specs=[pl.BlockSpec(memory_space=pltpu.SMEM)] + [hbm] * 4 + [vmem] * 2,
+        functools.partial(mixer_kernel, n, ring),
+        in_specs=[pl.BlockSpec(memory_space=pltpu.SMEM)] + [hbm] * 4 + [vmem] * 3,
         out_specs=[hbm] * 9 + [vmem] * 2,
         out_shape=[
             stack(d, F32), stack(d, F32), stack(d, BF16), stack(di, BF16), stack(wide, BF16), stack(d, BF16),
@@ -496,12 +632,18 @@
             pltpu.VMEM((rows, rows), F32),
             pltpu.VMEM((rows, rows), F32),
             pltpu.VMEM((2, rows, LANE), F32),
+            pltpu.VMEM(par.shape, F32),
+            pltpu.VMEM((n, *small.shape), F32),
             pltpu.SemaphoreType.DMA((2 * micros,)),
-            pltpu.SemaphoreType.DMA((wide // IN_TILE + 1,)),
+            pltpu.SemaphoreType.DMA((2,)),
             pltpu.SemaphoreType.DMA((3,)),
             pltpu.SemaphoreType.DMA((6,)),
             pltpu.SemaphoreType.DMA((micros, hands)),
             pltpu.SemaphoreType.DMA((micros, hands)),
+            pltpu.SemaphoreType.DMA((2, 2, steps, 2)),
+            pltpu.SemaphoreType.DMA((2, 2, steps, 2)),
+            pltpu.SemaphoreType.DMA((n,)),
+            pltpu.SemaphoreType.DMA((n,)),
         ],
         compiler_params=pltpu.CompilerParams(
             collective_id=1, has_side_effects=True, vmem_limit_bytes=MIXER_VMEM
@@ -510,26 +652,7 @@
             flops=12 * rows * d * (wide + di), bytes_accessed=100 << 20, transcendentals=16 << 20
         ),
         name="mixer_steps",
-    )(ends, x_in, cot, w_in, w_out_t, par, hp)
-
-
-def ring_place(index, n):
-    chip, core = index // 2, index % 2
-    z, x = chip // 2, chip % 2
-    return 2 * ((1 - x) * z + x * (n // 2 - 1 - z)) + core
-
-
-def ring_device(place, n):
-    spot, core = place // 2, place % 2
-    far = spot // (n // 4)
-    chip = (1 - far) * (2 * spot) + far * (2 * (n // 2 - 1 - spot) + 1)
-    return 2 * chip + core
-
-
-def tile_chunks(columns, parts):
-    tiles = columns // LANE
-    cuts = [LANE * (-(-tiles * i // parts)) for i in range(parts + 1)]
-    return [(cuts[i], cuts[i + 1] - cuts[i]) for i in range(parts)]
+    )(ends, x_in, cot, w_in, w_out_t, par, small, hp)
 
 
 def greet_all(n, me, section):
@@ -721,42 +844,55 @@
     cw = cw_piece * devices
     pad = LANE - heads
 
-    small = jnp.concatenate(
-        [norm_pre[0], conv_b[0], norm_gate[0], conv_w[0].reshape(-1)]
-    )
-    small = jnp.pad(small, (0, piece * pad - small.shape[0])).reshape(piece, pad)
-    gathered_in = lax.all_gather(jnp.concatenate([w_in[0], small], axis=1), "dp", axis=0, tiled=True)
-    gathered_out = lax.all_gather(w_out[0].T, "dp", axis=0, tiled=True)
-    tails = gathered_in[:, wide:].reshape(devices, piece * pad).astype(F32)
-    ends = [0]
-    for size in (piece, cw_piece, gate_piece, taps * cw_piece):
-        ends.append(ends[-1] + size)
-    gain_pre = tails[:, ends[0] : ends[1]].reshape(-1)
-    conv_bias = tails[:, ends[1] : ends[2]].reshape(-1)
-    gate_gain = tails[:, ends[2] : ends[3]].reshape(-1)
-    conv_taps = tails[:, ends[3] : ends[4]].reshape(devices, taps, cw_piece)
-    conv_taps = conv_taps.transpose(1, 0, 2).reshape(taps, cw)
-
-    def wide_row(v):
-        return jnp.pad(v, (0, cw - v.shape[0]))[None]
-
-    par = jnp.concatenate(
-        [
-            conv_taps,
-            conv_bias[None],
-            wide_row(gate_gain),
-            wide_row(jnp.repeat(skip_scale[0], di // heads)),
-            wide_row(gain_pre),
-        ],
-        axis=0,
-    )
+    ring = piece % 32 == 0 and devices % 4 == 0 and devices >= 12
+    skip_row = jnp.repeat(skip_scale[0], di // heads)
+
+    def wide_row(v, width):
+        return jnp.pad(v, (0, width - v.shape[0]))[None]
+
+    if ring:
+        shard_in = jnp.pad(w_in[0], ((0, 0), (0, pad)))
+        shard_out = w_out[0].T
+        small = jnp.concatenate(
+            [
+                conv_w[0],
+                conv_b,
+                wide_row(norm_gate[0], cw_piece),
+                jnp.zeros((1, cw_piece), BF16),
+                wide_row(norm_pre[0], cw_piece),
+            ],
+            axis=0,
+        ).astype(F32)
+        small = jnp.pad(small, ((0, 0), (0, -cw_piece % LANE)))
+        par = jnp.pad(skip_row[None], ((6, 1), (0, cw - di)))
+    else:
+        small = jnp.concatenate([norm_pre[0], conv_b[0], norm_gate[0], conv_w[0].reshape(-1)])
+        small = jnp.pad(small, (0, piece * pad - small.shape[0])).reshape(piece, pad)
+        shard_in = lax.all_gather(jnp.concatenate([w_in[0], small], axis=1), "dp", axis=0, tiled=True)
+        shard_out = lax.all_gather(w_out[0].T, "dp", axis=0, tiled=True)
+        tails = shard_in[:, wide:].reshape(devices, piece * pad).astype(F32)
+        cuts = [0]
+        for size in (piece, cw_piece, gate_piece, taps * cw_piece):
+            cuts.append(cuts[-1] + size)
+        conv_taps = tails[:, cuts[3] : cuts[4]].reshape(devices, taps, cw_piece)
+        par = jnp.concatenate(
+            [
+                conv_taps.transpose(1, 0, 2).reshape(taps, cw),
+                tails[:, cuts[1] : cuts[2]].reshape(1, -1),
+                wide_row(tails[:, cuts[2] : cuts[3]].reshape(-1), cw),
+                wide_row(skip_row, cw),
+                wide_row(tails[:, cuts[0] : cuts[1]].reshape(-1), cw),
+            ],
+            axis=0,
+        )
+        small = jnp.zeros((8, LANE), F32)
     hp = jnp.pad(jnp.stack([dt_bias[0], -jnp.exp(a_log[0])]), ((0, 6), (0, pad)))
 
     first_end = lengths[:, 0, 0]
     second_end = first_end + lengths[:, 0, 1]
     ends = jnp.stack([first_end, second_end], axis=1)
     (outputs, in_grad, normed_in, normed_out, grad_proj, grad_branch, _, _, _, packs, stats) = mixer_steps(
-        ends, x_in, cotangent, gathered_in, gathered_out, par, hp
+        devices, ring, ends, x_in, cotangent, shard_in, shard_out, par, small, hp
     )
     valid_total = jnp.sum(second_end).astype(F32)
 

time: 607 us -> 556 us (0.916)
  waiting for transfers between devices: 185 us -> 0 us
  Pallas kernels: 365 us -> 513 us
  between operations: 15.6 us -> 2.07 us
    all_gather x2 -> x0, waiting for transfers between devices: 184 us -> none  [the longest x1 104 us: shards(): lax.all_gather(jnp.concatenate([w_in[0], small], axis=1), 'dp', axis=0, t...]
    pallas_call x1, Pallas kernels: 205 us -> 347 us  [mixer_steps(): pl.pallas_call(functools.partial(mixer_kernel, n, ring), in_specs=[pl.Blo...]
  transfers between devices with their start and end apart: 2 -> 0, of which waited for: 2 -> 0; matrix products, arithmetic and copies ran while one was open for 1% -> 0% of each run, Pallas kernels for 0% -> 0%
where the time goes in v4:
time: 556 us; the launch traced here: 555 us
  Pallas kernels  513 us (92%)
  local copies, waits for them, and re-layouts  33.6 us (6%)
  other arithmetic  6.71 us (1%)
    pallas_call x1, Pallas kernels, mixer_steps(): pl.pallas_call(functools.partial(mixer_kernel, n, ring), in_specs=[pl.Blo...  347 us
    pallas_call x1, Pallas kernels, scatter_gradients(): pl.pallas_call(functools.partial(scatter_kernel, n), out_shape=[jax.Shape...  166 us

profile of v4, /device:TPU:0, one launch (start us, length us, event | category | flops | bytes accessed | tf_op | source)
XLA Modules:
  0.0 554.9 jit_solution(7077645333409216282)
XLA Ops:
  0.6 0.7 pad.33
  2.0 0.7 reduce.1
  2.7 0.7 concatenate.9
  3.4 1.5 add_reduce_fusion
  6.2 1.3 select_maximum_fusion.hp_ref
  8.1 0.7 broadcast_in_dim.51
  8.9 0.7 pad.31.par_in
  9.5 2.4 pad.30.win_hbm
  11.9 346.9 %mixer_steps.1 = (f32[2,256,1536]{2,1,0:T(8,128)}, f32[2,256,1536]{2,1,0:T(8,128)}, bf16[2,256,1536]{2,1,0:T(8,128)(2,1)}, bf16[2,256,3072]{2,1,0:T(8,128)(2,1)}...) custom-call(s32[2,2]{1,0:T(2,128)} %pad_add_fusion.ends, ...), custom_call_target="tpu_custom_call" | custom-call | flops 45298483200 | bytes 104857600 | tf_op jit(solution)/shard_map/mixer_steps/pallas_call | solution.py:598
  358.9 0.8 slice_bitcast_fusion.5
  359.7 0.7 slice_bitcast_fusion.6
  360.4 0.8 slice_reduce_fusion.3
  361.3 0.9 slice_reduce_fusion
  362.3 1.0 slice_reduce_fusion.1
  363.4 0.9 slice.65
  365.0 0.7 copy.36
  365.7 2.6 copy.33
  368.3 1.6 copy.34
  369.8 165.6 %gradient_scatter.1 = (f32[96,6528]{1,0:T(8,128)}, f32[96,3072]{1,0:T(8,128)}, f32[16,128]{1,0:T(8,128)}) custom-call(bf16[16,96,512]{2,1,0:T(8,128)(2,1)} %bitcast.53, bf16[16,96,512]{2,1,0:T(8,128)(2,1)} %bitcast.54, bf16[2,256,6528]{2,1,0:T(8,128)(2,1)} %get-tuple-element.27.gproj_hbm, bf16[2,256,3072]{2,1,0:T(8,128)(2,1)} %get-tuple-element.28.nout_hbm, ...), custom_call_target="tpu_custom_call" | custom-call | flops 15099494400 | bytes 20971520 | tf_op jit(solution)/shard_map/gradient_scatter/pallas_call | solution.py:804
  535.4 1.3 slice.91
  537.3 1.3 fusion.1
  538.6 1.3 slice_bitcast_fusion.4
  539.9 1.3 slice.89
  541.2 1.3 slice.85
  542.5 1.4 slice_bitcast_fusion.1
  543.9 0.7 slice.84
  544.6 0.7 reshape.79
  545.3 3.5 slice_bitcast_fusion
  548.7 1.7 copy.40
  550.4 1.4 copy-done
  551.8 1.7 copy.41
  553.9 1.0 copy.42
  (28 shorter events, 3.3 us)
Async XLA Ops:
  358.9 9.4 %copy-start.2 = (bf16[2,256,1536]{2,1,0:T(8,128)(2,1)S(1)}, bf16[2,256,1536]{2,1,0:T(8,128)(2,1)}, u32[]{:S(2)}) copy-start(bf16[2,256,1536]{2,1,0:T(8,128)(2,1)} %get-tuple-element.26) | copy-start | bytes 4718596
  545.3 3.5 copy-start.1
  548.7 3.0 copy-start
  551.8 2.1 copy-start.3
